TPU v7x, 32 devices: a whole 2x2x4 slice. The times are simulated.
32 devices in a mesh: parts: 2 (over y), slab: 4 (over z), section: 2 (over x), col: 2 (over core).
Axes of the slice: x: 2, y: 2, z: 4, core: 2. Of those that a mesh axis runs over, the one named last changes fastest.
Arguments:
- material_share: float32 [32, 256, 256], P(('parts', 'slab'), 'col', 'section'), parts along dimension 0, may hold values from 0.05 to 1
- stored_thermal_state: float32 [8, 16, 256, 256], P(('parts', 'section'), 'slab', 'col'), parts along dimension 0, may hold values from -6 to 6
- objective_slope: float32 [8, 16, 256, 256], P(('parts', 'section'), 'slab', 'col'), parts along dimension 0, may hold values from -6 to 6
- print_depths: int32 [8], P(('parts', 'section')), parts along dimension 0, may hold values from 1 to 16, as said below
- slice_to_deposit: int32 [32], P('parts'), parts along dimension 0, may hold values from 0 to 15, each once
Outputs:
- costate_temp: float32 [8, 16, 256, 256], P(('parts', 'section'), 'slab', 'col'), parts along dimension 0
- sensitivity: float32 [32, 256, 256], P(('parts', 'slab'), 'col', 'section'), parts along dimension 0
There are 2 independent parts, one for each index of `parts`. A program takes and returns all parts, laid end to end along the dimension named above; each array names one. Nothing has to cross between parts.
Inputs may be any that keep to these rules, and one draw needn't show every extreme that they name: `print_depths`: the planes present at a section are those whose build layer is under its height; in every draw some section has all 16 layers and some section only one. `slice_to_deposit`: every layer number appears at exactly one plane.
All inputs are finite; a program needn't handle non-finite values.
Results may differ from a plain program's by a relative error of at most 0.0003.
Values sent between devices are 32-bit elements; how exact they have to be, the bound alone decides.
A program may use at most 64 MiB of HBM per device.

v0:
```python
import jax
import jax.numpy as jnp
from jax import lax
from jax.sharding import PartitionSpec as P

SWEEPS = 6


LOSS_RATE = 0.05
FLOOR_COND = 0.001
SIMP_POWER = 3.0
BOUND_LOW = 0.05
BOUND_HIGH = 2.0


def with_halo(cells, sides, width):
    for axis, dim in sides:
        count = lax.axis_size(axis)
        ends = count - 1
        head = lax.slice_in_dim(cells, 0, width, axis=dim)
        tail = lax.slice_in_dim(cells, cells.shape[dim] - width, cells.shape[dim], axis=dim)
        cells = jnp.concatenate(
            [
                lax.ppermute(tail, axis, [(i, (i + 1) % count) for i in range(ends)]),
                cells,
                lax.ppermute(head, axis, [((i + 1) % count, i) for i in range(ends)]),
            ],
            axis=dim,
        )
    return cells


def conduct(material_share):
    return FLOOR_COND + (1.0 - FLOOR_COND) * material_share**3


def crop(tensor, pad_have, pad_want):
    offset = pad_have - pad_want
    if offset == 0:
        return tensor
    return tensor[:, offset : tensor.shape[1] - offset, offset : tensor.shape[2] - offset]


def section_faces(conduction, active):
    z_inner = 0.5 * active[:, 1:] * active[:, :-1] * (conduction[1:] + conduction[:-1])
    y_inner = 0.5 * active[:, :, 1:] * active[:, :, :-1] * (conduction[:, 1:] + conduction[:, :-1])
    x_inner = (
        0.5 * active[..., 1:] * active[..., :-1] * (conduction[:, :, 1:] + conduction[:, :, :-1])
    )
    z_face = jnp.pad(z_inner, ((0, 0), (1, 0), (0, 0), (0, 0)))
    y_face = jnp.pad(y_inner, ((0, 0), (0, 0), (1, 0), (0, 0)))
    x_face = jnp.pad(x_inner, ((0, 0), (0, 0), (0, 0), (1, 1)))
    z_upper = jnp.pad(z_face[:, 1:], ((0, 0), (0, 1), (0, 0), (0, 0)))
    y_upper = jnp.pad(y_face[:, :, 1:], ((0, 0), (0, 0), (0, 1), (0, 0)))
    diagonal = (
        LOSS_RATE * active
        + (1.0 - active)
        + z_face
        + z_upper
        + y_face
        + y_upper
        + x_face[..., :-1]
        + x_face[..., 1:]
    )
    return (z_face, y_face, x_face, diagonal)


def operate(adjoint_field, field_depth, rim_width, face_set):
    z_face, y_face, x_face, diagonal = face_set
    offset = rim_width - field_depth + 1
    plane_count = adjoint_field.shape[1] - 2
    row_count = adjoint_field.shape[2] - 2

    def window(tensor, plane_step, row_step):
        return tensor[
            :,
            offset + plane_step : offset + plane_step + plane_count,
            offset + row_step : offset + row_step + row_count,
        ]

    middle = adjoint_field[:, 1:-1, 1:-1]
    sideways = jnp.pad(middle, ((0, 0), (0, 0), (0, 0), (1, 1)))
    x_window = window(x_face, 0, 0)
    return (
        window(diagonal, 0, 0) * middle
        - window(z_face, 0, 0) * adjoint_field[:, :-2, 1:-1]
        - window(z_face, 1, 0) * adjoint_field[:, 2:, 1:-1]
        - window(y_face, 0, 0) * adjoint_field[:, 1:-1, :-2]
        - window(y_face, 0, 1) * adjoint_field[:, 1:-1, 2:]
        - x_window[..., :-1] * sideways[..., :-2]
        - x_window[..., 1:] * sideways[..., 2:]
    )


def face_energy(adjoint_wide, temp_wide, active_wide):
    z_term = (
        0.5
        * active_wide[:, 1:]
        * active_wide[:, :-1]
        * (adjoint_wide[:, 1:] - adjoint_wide[:, :-1])
        * (temp_wide[:, 1:] - temp_wide[:, :-1])
    )
    y_term = (
        0.5
        * active_wide[:, :, 1:]
        * active_wide[:, :, :-1]
        * (adjoint_wide[:, :, 1:] - adjoint_wide[:, :, :-1])
        * (temp_wide[:, :, 1:] - temp_wide[:, :, :-1])
    )
    adjoint_mid = adjoint_wide[:, 1:-1, 1:-1]
    temp_mid = temp_wide[:, 1:-1, 1:-1]
    active_mid = active_wide[:, 1:-1, 1:-1]
    x_term = (
        0.5
        * active_mid[..., 1:]
        * active_mid[..., :-1]
        * (adjoint_mid[..., 1:] - adjoint_mid[..., :-1])
        * (temp_mid[..., 1:] - temp_mid[..., :-1])
    )
    x_term = jnp.pad(x_term, ((0, 0), (0, 0), (0, 0), (1, 1)))
    z_sum = (z_term[:, :-1] + z_term[:, 1:])[:, :, 1:-1]
    y_sum = (y_term[:, :, :-1] + y_term[:, :, 1:])[:, 1:-1]
    return z_sum + y_sum + (x_term[..., :-1] + x_term[..., 1:])


def widen_single(adjoint_field):
    return with_halo(adjoint_field, (("slab", 1), ("col", 2)), 1)


def body(material_share, stored_thermal_state, objective_slope, print_depths, slice_to_deposit):
    step_indices, slice_indices, line_totals, voxel_indices = stored_thermal_state.shape
    rim_width = 1
    full_material_share = lax.all_gather(material_share, "section", axis=2, tiled=True)
    gathered_terms = jnp.concatenate(
        [full_material_share[None], stored_thermal_state, objective_slope], axis=0
    )
    extended = with_halo(gathered_terms, (("slab", 1), ("col", 2)), rim_width)
    conduction = conduct(extended[0])
    temp_wide = extended[1 : 1 + step_indices]
    grad_wide = extended[1 + step_indices :]
    plane_ids = (
        lax.axis_index("slab") * slice_indices
        - rim_width
        + jnp.arange(slice_indices + 2 * rim_width, dtype=jnp.int32)
    )
    row_ids = (
        lax.axis_index("col") * line_totals
        - rim_width
        + jnp.arange(line_totals + 2 * rim_width, dtype=jnp.int32)
    )
    total_planes = slice_to_deposit.shape[0]
    total_rows = line_totals * lax.axis_size("col")
    matches = plane_ids[:, None] == jnp.arange(total_planes, dtype=jnp.int32)[None, :]
    layers = jnp.sum(
        jnp.where(matches, slice_to_deposit[None, :], jnp.zeros_like(slice_to_deposit)[None, :]),
        axis=1,
    )
    inside_planes = (plane_ids >= 0) & (plane_ids < total_planes)
    inside_rows = (row_ids >= 0) & (row_ids < total_rows)
    live_layers = (layers[None, :] < print_depths[:, None]) & inside_planes[None, :]
    active = jnp.broadcast_to(
        (live_layers[:, :, None, None] & inside_rows[None, None, :, None]).astype(jnp.float32),
        (step_indices, slice_indices + 2 * rim_width, line_totals + 2 * rim_width, voxel_indices),
    )
    face_set = section_faces(conduction, active)
    diagonal = face_set[3]
    source = active * grad_wide
    center = 0.5 * (BOUND_HIGH + BOUND_LOW)
    half_width = 0.5 * (BOUND_HIGH - BOUND_LOW)
    cheb_ratio = center / half_width
    update = (
        crop(source, rim_width, rim_width - 1) / crop(diagonal, rim_width, rim_width - 1) / center
    )
    adjoint_field = update
    field_depth = rim_width - 1
    update_depth = rim_width - 1
    factor = 1.0 / cheb_ratio
    for sweep_index in range(1, SWEEPS):
        adjoint_field = widen_single(adjoint_field)
        field_depth = 1
        residue = crop(source, rim_width, field_depth - 1) - operate(
            adjoint_field, field_depth, rim_width, face_set
        )
        factor_next = 1.0 / (2.0 * cheb_ratio - factor)
        update = factor_next * factor * crop(
            update, update_depth, field_depth - 1
        ) + 2.0 * factor_next / half_width * (residue / crop(diagonal, rim_width, field_depth - 1))
        adjoint_field = crop(adjoint_field, field_depth, field_depth - 1) + update
        field_depth = field_depth - 1
        update_depth = field_depth
        factor = factor_next
    adjoint_field = widen_single(adjoint_field)
    field_depth = 1
    energy = face_energy(
        crop(adjoint_field, field_depth, 1),
        crop(temp_wide, rim_width, 1),
        crop(active, rim_width, 1),
    )
    slope_rho = (1.0 - FLOOR_COND) * SIMP_POWER * full_material_share * full_material_share
    local_term = -slope_rho * jnp.sum(energy, axis=0)
    sensitivity = lax.psum_scatter(local_term, "section", scatter_dimension=2, tiled=True)
    return (crop(adjoint_field, field_depth, 0), sensitivity)


def solution(mesh):
    return jax.shard_map(
        body,
        mesh=mesh,
        in_specs=(
            P(("parts", "slab"), "col", "section"),
            P(("parts", "section"), "slab", "col", None),
            P(("parts", "section"), "slab", "col", None),
            P(("parts", "section")),
            P("parts"),
        ),
        out_specs=(
            P(("parts", "section"), "slab", "col", None),
            P(("parts", "slab"), "col", "section"),
        ),
        check_vma=False,
    )
```

profile of v0, /device:TPU:0, one launch (start us, length us, event | category | flops | bytes accessed | tf_op | source)
XLA Modules:
  0.0 191.5 jit_solution(18190951621507992088)
XLA Ops:
  7.2 10.2 %all_gather.3 = f32[4,128,256]{2,1,0:T(8,128)S(1)} all-gather(f32[4,128,128]{2,1,0:T(8,128)} %param.5), channel_id=1, replica_groups=mesh['parts'=2,'slab'=4,'section'=2,'col'=2] {'section'}, dimensions={2}, use_global_device_ids=true | all-gather | bytes 786432 | tf_op jit(solution)/shard_map/all_gather | solution.py:133
  17.4 2.6 %pad_maximum_fusion.54 = (f32[5,1,128,256]{3,2,1,0:T(8,128)}, f32[5,1,128,256]{3,2,1,0:T(8,128)}) fusion(f32[2,4,128,256]{3,2,1,0:T(8,128)} %param.7, f32[2,4,128,256]{3,2,1,0:T(8,128)} %param.6, f32[1,4,128,256]{3,2,1,0:T(8,128)S(1)} %bitcast.5), kind=kLoop, calls=%fused_computation.186 | loop fusion | flops 655360 | bytes 3932160 | tf_op jit(solution)/shard_map/slice | solution.py:21
  20.0 4.5 %collective-permute-start = (f32[5,1,128,256]{3,2,1,0:T(8,128)}, f32[5,1,128,256]{3,2,1,0:T(8,128)}, u32[]{:S(2)}, u32[]{:S(2)}) collective-permute-start(f32[5,1,128,256]{3,2,1,0:T(8,128)} %get-tuple-element.14), channel_id=1, source_target_pairs={{0,4},{4,8},{8,12},{1,5},{5,9},{9,13},{2,6},{6,10},{10,14},{3,7},{... | collective-permute-start | bytes 1966088 | tf_op jit(solution)/shard_map/ppermute | solution.py:24
  26.4 10.7 %collective-permute-done = f32[5,1,128,256]{3,2,1,0:T(8,128)} collective-permute-done((f32[5,1,128,256]{3,2,1,0:T(8,128)}, f32[5,1,128,256]{3,2,1,0:T(8,128)}, u32[]{:S(2)}, u32[]{:S(2)}) %collective-permute-start) | collective-permute-done | bytes 655392 | tf_op jit(solution)/shard_map/ppermute | solution.py:24
  37.1 4.9 %collective-permute-done.1 = f32[5,1,128,256]{3,2,1,0:T(8,128)} collective-permute-done((f32[5,1,128,256]{3,2,1,0:T(8,128)}, f32[5,1,128,256]{3,2,1,0:T(8,128)}, u32[]{:S(2)}, u32[]{:S(2)}) %collective-permute-start.1) | collective-permute-done | bytes 655392 | tf_op jit(solution)/shard_map/ppermute | solution.py:26
  44.2 1.3 collective-permute-start.3
  45.7 1.6 collective-permute-done.3
  49.8 1.8 pad_maximum_fusion
  53.2 2.7 %collective-permute-start.4 = (f32[2,1,128,256]{3,2,1,0:T(8,128)S(1)}, f32[2,1,128,256]{3,2,1,0:T(8,128)S(1)}, u32[]{:S(2)}, u32[]{:S(2)}) collective-permute-start(f32[2,1,128,256]{3,2,1,0:T(8,128)S(1)} %get-tuple-element.44), channel_id=1, source_target_pairs={{0,4},{4,8},{8,12},{1,5},{5,9},{9,13},{2,6},{6,10},{10,14},{3,7},{... | collective-permute-start | bytes 786440 | tf_op jit(solution)/shard_map/ppermute | solution.py:24
  55.9 1.3 collective-permute-start.5
  57.2 4.6 %collective-permute-done.4 = f32[2,1,128,256]{3,2,1,0:T(8,128)S(1)} collective-permute-done((f32[2,1,128,256]{3,2,1,0:T(8,128)S(1)}, f32[2,1,128,256]{3,2,1,0:T(8,128)S(1)}, u32[]{:S(2)}, u32[]{:S(2)}) %collective-permute-start.4) | collective-permute-done | bytes 262176 | tf_op jit(solution)/shard_map/ppermute | solution.py:24
  61.8 4.1 %collective-permute-done.5 = f32[2,1,128,256]{3,2,1,0:T(8,128)S(1)} collective-permute-done((f32[2,1,128,256]{3,2,1,0:T(8,128)S(1)}, f32[2,1,128,256]{3,2,1,0:T(8,128)S(1)}, u32[]{:S(2)}, u32[]{:S(2)}) %collective-permute-start.5) | collective-permute-done | bytes 262176 | tf_op jit(solution)/shard_map/ppermute | solution.py:26
  67.2 1.3 collective-permute-start.7
  68.5 1.8 collective-permute-done.7
  70.3 2.1 %fusion.97 = (f32[2,4,128,256]{3,2,1,0:T(8,128)S(1)}, f32[2,4,128,256]{3,2,1,0:T(8,128)S(1)}) fusion(f32[2,4,128,256]{3,2,1,0:T(8,128)S(1)} %get-tuple-element.11, f32[2,6,130,256]{3,2,1,0:T(8,128)S(1)} %slice.508, f32[2,4,128]{2,1,0:T(4,128)S(1)} %get-tuple-element.47, f32[2,4,128,256]{3,2,1,0:T(8,128)S(1)} %get-tuple-element.10, ...), kind=kLoop, calls=%fused_computation.191 | loop fusion | flops 7864320 | bytes 11581344 | tf_op jit(solution)/shard_map/add | solution.py:188
  72.5 3.5 %collective-permute-start.8 = (f32[2,1,128,256]{3,2,1,0:T(8,128)S(1)}, f32[2,1,128,256]{3,2,1,0:T(8,128)S(1)}, u32[]{:S(2)}, u32[]{:S(2)}) collective-permute-start(f32[2,1,128,256]{3,2,1,0:T(8,128)S(1)} %get-tuple-element.42), channel_id=1, source_target_pairs={{0,4},{4,8},{8,12},{1,5},{5,9},{9,13},{2,6},{6,10},{10,14},{3,7},{... | collective-permute-start | bytes 786440 | tf_op jit(solution)/shard_map/ppermute | solution.py:24
  76.0 1.3 collective-permute-start.9
  77.3 4.6 %collective-permute-done.8 = f32[2,1,128,256]{3,2,1,0:T(8,128)S(1)} collective-permute-done((f32[2,1,128,256]{3,2,1,0:T(8,128)S(1)}, f32[2,1,128,256]{3,2,1,0:T(8,128)S(1)}, u32[]{:S(2)}, u32[]{:S(2)}) %collective-permute-start.8) | collective-permute-done | bytes 262176 | tf_op jit(solution)/shard_map/ppermute | solution.py:24
  81.8 4.1 %collective-permute-done.9 = f32[2,1,128,256]{3,2,1,0:T(8,128)S(1)} collective-permute-done((f32[2,1,128,256]{3,2,1,0:T(8,128)S(1)}, f32[2,1,128,256]{3,2,1,0:T(8,128)S(1)}, u32[]{:S(2)}, u32[]{:S(2)}) %collective-permute-start.9) | collective-permute-done | bytes 262176 | tf_op jit(solution)/shard_map/ppermute | solution.py:26
  87.3 1.3 collective-permute-start.11
  88.6 1.8 collective-permute-done.11
  90.4 2.2 %fusion.105 = (f32[2,4,128,256]{3,2,1,0:T(8,128)S(1)}, f32[2,4,128,256]{3,2,1,0:T(8,128)S(1)}) fusion(f32[2,4,128,256]{3,2,1,0:T(8,128)S(1)} %get-tuple-element.8, f32[2,4,128,256]{3,2,1,0:T(8,128)S(1)} %get-tuple-element.11, f32[2,6,130,255]{3,2,1,0:T(8,128)S(1)} %broadcast_multiply_fusion, f32[2,6,1,256]{3,2,1,0:T(1,128)S(1)} %collective-permute-done.11, ...), kind=kLoop, calls=%fused_computation.233 | loop fusion | flops 7340032 | bytes 12629920 | tf_op jit(solution)/shard_map/add | solution.py:188
  92.6 2.2 %collective-permute-start.12 = (f32[2,1,128,256]{3,2,1,0:T(8,128)S(1)}, f32[2,1,128,256]{3,2,1,0:T(8,128)S(1)}, u32[]{:S(2)}, u32[]{:S(2)}) collective-permute-start(f32[2,1,128,256]{3,2,1,0:T(8,128)S(1)} %get-tuple-element.40), channel_id=1, source_target_pairs={{0,4},{4,8},{8,12},{1,5},{5,9},{9,13},{2,6},{6,10},{10,14},{3,7},{... | collective-permute-start | bytes 786440 | tf_op jit(solution)/shard_map/ppermute | solution.py:24
  94.8 1.3 collective-permute-start.13
  96.1 4.6 %collective-permute-done.12 = f32[2,1,128,256]{3,2,1,0:T(8,128)S(1)} collective-permute-done((f32[2,1,128,256]{3,2,1,0:T(8,128)S(1)}, f32[2,1,128,256]{3,2,1,0:T(8,128)S(1)}, u32[]{:S(2)}, u32[]{:S(2)}) %collective-permute-start.12) | collective-permute-done | bytes 262176 | tf_op jit(solution)/shard_map/ppermute | solution.py:24
  100.7 4.1 %collective-permute-done.13 = f32[2,1,128,256]{3,2,1,0:T(8,128)S(1)} collective-permute-done((f32[2,1,128,256]{3,2,1,0:T(8,128)S(1)}, f32[2,1,128,256]{3,2,1,0:T(8,128)S(1)}, u32[]{:S(2)}, u32[]{:S(2)}) %collective-permute-start.13) | collective-permute-done | bytes 262176 | tf_op jit(solution)/shard_map/ppermute | solution.py:26
  106.1 1.3 collective-permute-start.15
  107.5 1.8 collective-permute-done.15
  109.2 2.2 %fusion.103 = (f32[2,4,128,256]{3,2,1,0:T(8,128)S(1)}, f32[2,4,128,256]{3,2,1,0:T(8,128)S(1)}) fusion(f32[2,4,128,256]{3,2,1,0:T(8,128)S(1)} %get-tuple-element.6, f32[2,4,128,256]{3,2,1,0:T(8,128)S(1)} %get-tuple-element.11, f32[2,6,130,255]{3,2,1,0:T(8,128)S(1)} %broadcast_multiply_fusion, f32[2,6,1,256]{3,2,1,0:T(1,128)S(1)} %collective-permute-done.15, ...), kind=kLoop, calls=%fused_computation.232 | loop fusion | flops 7340032 | bytes 12629920 | tf_op jit(solution)/shard_map/add | solution.py:188
  111.4 2.2 %collective-permute-start.16 = (f32[2,1,128,256]{3,2,1,0:T(8,128)S(1)}, f32[2,1,128,256]{3,2,1,0:T(8,128)S(1)}, u32[]{:S(2)}, u32[]{:S(2)}) collective-permute-start(f32[2,1,128,256]{3,2,1,0:T(8,128)S(1)} %get-tuple-element.38), channel_id=1, source_target_pairs={{0,4},{4,8},{8,12},{1,5},{5,9},{9,13},{2,6},{6,10},{10,14},{3,7},{... | collective-permute-start | bytes 786440 | tf_op jit(solution)/shard_map/ppermute | solution.py:24
  113.6 1.3 collective-permute-start.17
  114.9 4.6 %collective-permute-done.16 = f32[2,1,128,256]{3,2,1,0:T(8,128)S(1)} collective-permute-done((f32[2,1,128,256]{3,2,1,0:T(8,128)S(1)}, f32[2,1,128,256]{3,2,1,0:T(8,128)S(1)}, u32[]{:S(2)}, u32[]{:S(2)}) %collective-permute-start.16) | collective-permute-done | bytes 262176 | tf_op jit(solution)/shard_map/ppermute | solution.py:24
  119.5 4.1 %collective-permute-done.17 = f32[2,1,128,256]{3,2,1,0:T(8,128)S(1)} collective-permute-done((f32[2,1,128,256]{3,2,1,0:T(8,128)S(1)}, f32[2,1,128,256]{3,2,1,0:T(8,128)S(1)}, u32[]{:S(2)}, u32[]{:S(2)}) %collective-permute-start.17) | collective-permute-done | bytes 262176 | tf_op jit(solution)/shard_map/ppermute | solution.py:26
  124.9 1.3 collective-permute-start.19
  126.3 1.8 collective-permute-done.19
  128.0 2.2 %fusion.101 = (f32[2,4,128,256]{3,2,1,0:T(8,128)S(1)}, f32[2,4,128,256]{3,2,1,0:T(8,128)S(1)}) fusion(f32[2,4,128,256]{3,2,1,0:T(8,128)S(1)} %get-tuple-element.4, f32[2,4,128,256]{3,2,1,0:T(8,128)S(1)} %get-tuple-element.11, f32[2,6,130,255]{3,2,1,0:T(8,128)S(1)} %broadcast_multiply_fusion, f32[2,6,1,256]{3,2,1,0:T(1,128)S(1)} %collective-permute-done.19, ...), kind=kLoop, calls=%fused_computation.231 | loop fusion | flops 7340032 | bytes 12629920 | tf_op jit(solution)/shard_map/add | solution.py:188
  130.3 2.2 %collective-permute-start.20 = (f32[2,1,128,256]{3,2,1,0:T(8,128)S(1)}, f32[2,1,128,256]{3,2,1,0:T(8,128)S(1)}, u32[]{:S(2)}, u32[]{:S(2)}) collective-permute-start(f32[2,1,128,256]{3,2,1,0:T(8,128)S(1)} %get-tuple-element.36), channel_id=1, source_target_pairs={{0,4},{4,8},{8,12},{1,5},{5,9},{9,13},{2,6},{6,10},{10,14},{3,7},{... | collective-permute-start | bytes 786440 | tf_op jit(solution)/shard_map/ppermute | solution.py:24
  133.8 4.6 %collective-permute-done.20 = f32[2,1,128,256]{3,2,1,0:T(8,128)S(1)} collective-permute-done((f32[2,1,128,256]{3,2,1,0:T(8,128)S(1)}, f32[2,1,128,256]{3,2,1,0:T(8,128)S(1)}, u32[]{:S(2)}, u32[]{:S(2)}) %collective-permute-start.20) | collective-permute-done | bytes 262176 | tf_op jit(solution)/shard_map/ppermute | solution.py:24
  138.3 4.1 %collective-permute-done.21 = f32[2,1,128,256]{3,2,1,0:T(8,128)S(1)} collective-permute-done((f32[2,1,128,256]{3,2,1,0:T(8,128)S(1)}, f32[2,1,128,256]{3,2,1,0:T(8,128)S(1)}, u32[]{:S(2)}, u32[]{:S(2)}) %collective-permute-start.21) | collective-permute-done | bytes 262176 | tf_op jit(solution)/shard_map/ppermute | solution.py:26
  143.8 1.3 collective-permute-start.23
  145.1 1.8 collective-permute-done.23
  146.9 2.2 %fusion.44 = f32[2,4,128,256]{3,2,1,0:T(8,128)S(1)} fusion(f32[2,4,128,256]{3,2,1,0:T(8,128)S(1)} %get-tuple-element.2, f32[2,4,128,256]{3,2,1,0:T(8,128)S(1)} %get-tuple-element.11, f32[2,6,1,256]{3,2,1,0:T(1,128)S(1)} %collective-permute-done.23, f32[2,1,128,256]{3,2,1,0:T(8,128)S(1)} %collective-permute-done.21, ...), kind=kLoop, calls=%fused_computation.76 | loop fusion | flops 7340032 | bytes 11581344 | tf_op jit(solution)/shard_map/add | solution.py:188
  149.1 2.2 %collective-permute-start.24 = (f32[2,1,128,256]{3,2,1,0:T(8,128)S(1)}, f32[2,1,128,256]{3,2,1,0:T(8,128)S(1)}, u32[]{:S(2)}, u32[]{:S(2)}) collective-permute-start(f32[2,1,128,256]{3,2,1,0:T(8,128)S(1)} %get-tuple-element.34), channel_id=1, source_target_pairs={{0,4},{4,8},{8,12},{1,5},{5,9},{9,13},{2,6},{6,10},{10,14},{3,7},{... | collective-permute-start | bytes 786440 | tf_op jit(solution)/shard_map/ppermute | solution.py:24
  152.6 4.6 %collective-permute-done.24 = f32[2,1,128,256]{3,2,1,0:T(8,128)S(1)} collective-permute-done((f32[2,1,128,256]{3,2,1,0:T(8,128)S(1)}, f32[2,1,128,256]{3,2,1,0:T(8,128)S(1)}, u32[]{:S(2)}, u32[]{:S(2)}) %collective-permute-start.24) | collective-permute-done | bytes 262176 | tf_op jit(solution)/shard_map/ppermute | solution.py:24
  157.2 4.1 %collective-permute-done.25 = f32[2,1,128,256]{3,2,1,0:T(8,128)S(1)} collective-permute-done((f32[2,1,128,256]{3,2,1,0:T(8,128)S(1)}, f32[2,1,128,256]{3,2,1,0:T(8,128)S(1)}, u32[]{:S(2)}, u32[]{:S(2)}) %collective-permute-start.25) | collective-permute-done | bytes 262176 | tf_op jit(solution)/shard_map/ppermute | solution.py:26
  162.6 1.5 collective-permute-start.27
  167.2 2.7 %fusion.1 = f32[2,6,129,256]{3,2,1,0:T(8,128)S(1)} fusion(f32[5,6,1,256]{3,2,1,0:T(1,128)S(1)} %collective-permute-done.2, f32[5,1,128,256]{3,2,1,0:T(8,128)} %collective-permute-done.1, f32[5,1,128,256]{3,2,1,0:T(8,128)} %collective-permute-done, f32[2,4,128,256]{3,2,1,0:T(8,128)S(1)} %copy-done.2, f32[2,4,128,256]{3,2,1,0:T(8,128)S(1)} %copy-done, ...), kind=kLoop, calls=%fused_computation.19 | loop fusion | flops 7925760 | bytes 7182384 | tf_op jit(solution)/shard_map/mul | solution.py:104
  171.7 12.9 %reduce-scatter.2.cloned.1.call-done = f32[4,128,128]{2,1,0:T(8,128)} async-done(((f32[4,128,256]{2,1,0:T(8,128)}), f32[4,128,128]{2,1,0:T(8,128)}) %reduce-scatter.2.cloned.1.call-update) | async-done | bytes 262160 | tf_op jit(solution)/shard_map/reduce_scatter | solution.py:201
  (75 shorter events, 23.7 us)
Async XLA Ops:
  7.2 177.5 %reduce-scatter.2.cloned.1.call-start = ((), (), s32[]{:S(2)}) async-start(), calls=%async_computation.1 | async-start | bytes 786432 | tf_op jit(solution)/shard_map/reduce_scatter | solution.py:201
  17.4 32.4 %copy-start.3 = (f32[4,128,256]{2,1,0:T(8,128)}, f32[4,128,256]{2,1,0:T(8,128)S(1)}, u32[]{:S(2)}) copy-start(f32[4,128,256]{2,1,0:T(8,128)S(1)} %all_gather.3) | copy-start | bytes 1572868
  17.4 8.5 %copy-start.6 = (s32[16]{0:T(128)S(1)}, s32[16]{0:T(128)}, u32[]{:S(2)}) copy-start(s32[16]{0:T(128)} %param.9) | copy-start | bytes 196
  17.4 8.7 %copy-start.5 = (s32[2]{0:T(128)S(1)}, s32[2]{0:T(128)}, u32[]{:S(2)}) copy-start(s32[2]{0:T(128)} %param.8) | copy-start | bytes 28
  17.4 24.6 %copy-start = (f32[2,4,128,256]{3,2,1,0:T(8,128)S(1)}, f32[2,4,128,256]{3,2,1,0:T(8,128)}, u32[]{:S(2)}) copy-start(f32[2,4,128,256]{3,2,1,0:T(8,128)} %param.6) | copy-start | bytes 3145732
  17.4 24.6 %copy-start.2 = (f32[2,4,128,256]{3,2,1,0:T(8,128)S(1)}, f32[2,4,128,256]{3,2,1,0:T(8,128)}, u32[]{:S(2)}) copy-start(f32[2,4,128,256]{3,2,1,0:T(8,128)} %param.7) | copy-start | bytes 3145732
  20.0 17.1 %collective-permute-start = (f32[5,1,128,256]{3,2,1,0:T(8,128)}, f32[5,1,128,256]{3,2,1,0:T(8,128)}, u32[]{:S(2)}, u32[]{:S(2)}) collective-permute-start(f32[5,1,128,256]{3,2,1,0:T(8,128)} %get-tuple-element.14), channel_id=1, source_target_pairs={{0,4},{4,8},{8,12},{1,5},{5,9},{9,13},{2,6},{6,10},{10,14},{3,7},{... | collective-permute-start | bytes 1966088 | tf_op jit(solution)/shard_map/ppermute | solution.py:24
  24.5 17.5 %collective-permute-start.1 = (f32[5,1,128,256]{3,2,1,0:T(8,128)}, f32[5,1,128,256]{3,2,1,0:T(8,128)}, u32[]{:S(2)}, u32[]{:S(2)}) collective-permute-start(f32[5,1,128,256]{3,2,1,0:T(8,128)} %get-tuple-element.15), channel_id=1, source_target_pairs={{4,0},{8,4},{12,8},{5,1},{9,5},{13,9},{6,2},{10,6},{14,10},{7,3},{... | collective-permute-start | bytes 1966088 | tf_op jit(solution)/shard_map/ppermute | solution.py:26
  42.9 2.8 %collective-permute-start.2 = (f32[5,6,1,256]{3,2,1,0:T(1,128)S(1)}, f32[5,6,1,256]{3,2,1,0:T(1,128)S(1)}, u32[]{:S(2)}, u32[]{:S(2)}) collective-permute-start(f32[5,6,1,256]{3,2,1,0:T(1,128)S(1)} %get-tuple-element.12), channel_id=1, source_target_pairs={{0,1},{2,3},{4,5},{6,7},{8,9},{10,11},{12,13},{14,15},{16,17},{18,... | collective-permute-start | bytes 92168 | tf_op jit(solution)/shard_map/ppermute | solution.py:24
  44.2 3.1 %collective-permute-start.3 = (f32[5,6,1,256]{3,2,1,0:T(1,128)S(1)}, f32[5,6,1,256]{3,2,1,0:T(1,128)S(1)}, u32[]{:S(2)}, u32[]{:S(2)}) collective-permute-start(f32[5,6,1,256]{3,2,1,0:T(1,128)S(1)} %get-tuple-element.13), channel_id=1, source_target_pairs={{1,0},{3,2},{5,4},{7,6},{9,8},{11,10},{13,12},{15,14},{17,16},{19,... | collective-permute-start | bytes 92168 | tf_op jit(solution)/shard_map/ppermute | solution.py:26
  53.2 8.5 %collective-permute-start.4 = (f32[2,1,128,256]{3,2,1,0:T(8,128)S(1)}, f32[2,1,128,256]{3,2,1,0:T(8,128)S(1)}, u32[]{:S(2)}, u32[]{:S(2)}) collective-permute-start(f32[2,1,128,256]{3,2,1,0:T(8,128)S(1)} %get-tuple-element.44), channel_id=1, source_target_pairs={{0,4},{4,8},{8,12},{1,5},{5,9},{9,13},{2,6},{6,10},{10,14},{3,7},{... | collective-permute-start | bytes 786440 | tf_op jit(solution)/shard_map/ppermute | solution.py:24
  55.9 10.0 %collective-permute-start.5 = (f32[2,1,128,256]{3,2,1,0:T(8,128)S(1)}, f32[2,1,128,256]{3,2,1,0:T(8,128)S(1)}, u32[]{:S(2)}, u32[]{:S(2)}) collective-permute-start(f32[2,1,128,256]{3,2,1,0:T(8,128)S(1)} %get-tuple-element.45), channel_id=1, source_target_pairs={{4,0},{8,4},{12,8},{5,1},{9,5},{13,9},{6,2},{10,6},{14,10},{7,3},{... | collective-permute-start | bytes 786440 | tf_op jit(solution)/shard_map/ppermute | solution.py:26
  65.9 2.6 %collective-permute-start.6 = (f32[2,6,1,256]{3,2,1,0:T(1,128)S(1)}, f32[2,6,1,256]{3,2,1,0:T(1,128)S(1)}, u32[]{:S(2)}, u32[]{:S(2)}) collective-permute-start(f32[2,6,1,256]{3,2,1,0:T(1,128)S(1)} %get-tuple-element.30), channel_id=1, source_target_pairs={{0,1},{2,3},{4,5},{6,7},{8,9},{10,11},{12,13},{14,15},{16,17},{18,... | collective-permute-start | bytes 36872 | tf_op jit(solution)/shard_map/ppermute | solution.py:24
  67.2 3.1 %collective-permute-start.7 = (f32[2,6,1,256]{3,2,1,0:T(1,128)S(1)}, f32[2,6,1,256]{3,2,1,0:T(1,128)S(1)}, u32[]{:S(2)}, u32[]{:S(2)}) collective-permute-start(f32[2,6,1,256]{3,2,1,0:T(1,128)S(1)} %get-tuple-element.31), channel_id=1, source_target_pairs={{1,0},{3,2},{5,4},{7,6},{9,8},{11,10},{13,12},{15,14},{17,16},{19,... | collective-permute-start | bytes 36872 | tf_op jit(solution)/shard_map/ppermute | solution.py:26
  72.5 9.4 %collective-permute-start.8 = (f32[2,1,128,256]{3,2,1,0:T(8,128)S(1)}, f32[2,1,128,256]{3,2,1,0:T(8,128)S(1)}, u32[]{:S(2)}, u32[]{:S(2)}) collective-permute-start(f32[2,1,128,256]{3,2,1,0:T(8,128)S(1)} %get-tuple-element.42), channel_id=1, source_target_pairs={{0,4},{4,8},{8,12},{1,5},{5,9},{9,13},{2,6},{6,10},{10,14},{3,7},{... | collective-permute-start | bytes 786440 | tf_op jit(solution)/shard_map/ppermute | solution.py:24
  76.0 10.0 %collective-permute-start.9 = (f32[2,1,128,256]{3,2,1,0:T(8,128)S(1)}, f32[2,1,128,256]{3,2,1,0:T(8,128)S(1)}, u32[]{:S(2)}, u32[]{:S(2)}) collective-permute-start(f32[2,1,128,256]{3,2,1,0:T(8,128)S(1)} %get-tuple-element.43), channel_id=1, source_target_pairs={{4,0},{8,4},{12,8},{5,1},{9,5},{13,9},{6,2},{10,6},{14,10},{7,3},{... | collective-permute-start | bytes 786440 | tf_op jit(solution)/shard_map/ppermute | solution.py:26
  86.0 2.6 %collective-permute-start.10 = (f32[2,6,1,256]{3,2,1,0:T(1,128)S(1)}, f32[2,6,1,256]{3,2,1,0:T(1,128)S(1)}, u32[]{:S(2)}, u32[]{:S(2)}) collective-permute-start(f32[2,6,1,256]{3,2,1,0:T(1,128)S(1)} %get-tuple-element.28), channel_id=1, source_target_pairs={{0,1},{2,3},{4,5},{6,7},{8,9},{10,11},{12,13},{14,15},{16,17},{18,... | collective-permute-start | bytes 36872 | tf_op jit(solution)/shard_map/ppermute | solution.py:24
  87.3 3.1 %collective-permute-start.11 = (f32[2,6,1,256]{3,2,1,0:T(1,128)S(1)}, f32[2,6,1,256]{3,2,1,0:T(1,128)S(1)}, u32[]{:S(2)}, u32[]{:S(2)}) collective-permute-start(f32[2,6,1,256]{3,2,1,0:T(1,128)S(1)} %get-tuple-element.29), channel_id=1, source_target_pairs={{1,0},{3,2},{5,4},{7,6},{9,8},{11,10},{13,12},{15,14},{17,16},{19,... | collective-permute-start | bytes 36872 | tf_op jit(solution)/shard_map/ppermute | solution.py:26
  92.6 8.1 %collective-permute-start.12 = (f32[2,1,128,256]{3,2,1,0:T(8,128)S(1)}, f32[2,1,128,256]{3,2,1,0:T(8,128)S(1)}, u32[]{:S(2)}, u32[]{:S(2)}) collective-permute-start(f32[2,1,128,256]{3,2,1,0:T(8,128)S(1)} %get-tuple-element.40), channel_id=1, source_target_pairs={{0,4},{4,8},{8,12},{1,5},{5,9},{9,13},{2,6},{6,10},{10,14},{3,7},{... | collective-permute-start | bytes 786440 | tf_op jit(solution)/shard_map/ppermute | solution.py:24
  94.8 10.0 %collective-permute-start.13 = (f32[2,1,128,256]{3,2,1,0:T(8,128)S(1)}, f32[2,1,128,256]{3,2,1,0:T(8,128)S(1)}, u32[]{:S(2)}, u32[]{:S(2)}) collective-permute-start(f32[2,1,128,256]{3,2,1,0:T(8,128)S(1)} %get-tuple-element.41), channel_id=1, source_target_pairs={{4,0},{8,4},{12,8},{5,1},{9,5},{13,9},{6,2},{10,6},{14,10},{7,3},{... | collective-permute-start | bytes 786440 | tf_op jit(solution)/shard_map/ppermute | solution.py:26
  104.8 2.6 %collective-permute-start.14 = (f32[2,6,1,256]{3,2,1,0:T(1,128)S(1)}, f32[2,6,1,256]{3,2,1,0:T(1,128)S(1)}, u32[]{:S(2)}, u32[]{:S(2)}) collective-permute-start(f32[2,6,1,256]{3,2,1,0:T(1,128)S(1)} %get-tuple-element.26), channel_id=1, source_target_pairs={{0,1},{2,3},{4,5},{6,7},{8,9},{10,11},{12,13},{14,15},{16,17},{18,... | collective-permute-start | bytes 36872 | tf_op jit(solution)/shard_map/ppermute | solution.py:24
  106.1 3.1 %collective-permute-start.15 = (f32[2,6,1,256]{3,2,1,0:T(1,128)S(1)}, f32[2,6,1,256]{3,2,1,0:T(1,128)S(1)}, u32[]{:S(2)}, u32[]{:S(2)}) collective-permute-start(f32[2,6,1,256]{3,2,1,0:T(1,128)S(1)} %get-tuple-element.27), channel_id=1, source_target_pairs={{1,0},{3,2},{5,4},{7,6},{9,8},{11,10},{13,12},{15,14},{17,16},{19,... | collective-permute-start | bytes 36872 | tf_op jit(solution)/shard_map/ppermute | solution.py:26
  111.4 8.1 %collective-permute-start.16 = (f32[2,1,128,256]{3,2,1,0:T(8,128)S(1)}, f32[2,1,128,256]{3,2,1,0:T(8,128)S(1)}, u32[]{:S(2)}, u32[]{:S(2)}) collective-permute-start(f32[2,1,128,256]{3,2,1,0:T(8,128)S(1)} %get-tuple-element.38), channel_id=1, source_target_pairs={{0,4},{4,8},{8,12},{1,5},{5,9},{9,13},{2,6},{6,10},{10,14},{3,7},{... | collective-permute-start | bytes 786440 | tf_op jit(solution)/shard_map/ppermute | solution.py:24
  113.6 10.0 %collective-permute-start.17 = (f32[2,1,128,256]{3,2,1,0:T(8,128)S(1)}, f32[2,1,128,256]{3,2,1,0:T(8,128)S(1)}, u32[]{:S(2)}, u32[]{:S(2)}) collective-permute-start(f32[2,1,128,256]{3,2,1,0:T(8,128)S(1)} %get-tuple-element.39), channel_id=1, source_target_pairs={{4,0},{8,4},{12,8},{5,1},{9,5},{13,9},{6,2},{10,6},{14,10},{7,3},{... | collective-permute-start | bytes 786440 | tf_op jit(solution)/shard_map/ppermute | solution.py:26
  123.6 2.6 %collective-permute-start.18 = (f32[2,6,1,256]{3,2,1,0:T(1,128)S(1)}, f32[2,6,1,256]{3,2,1,0:T(1,128)S(1)}, u32[]{:S(2)}, u32[]{:S(2)}) collective-permute-start(f32[2,6,1,256]{3,2,1,0:T(1,128)S(1)} %get-tuple-element.24), channel_id=1, source_target_pairs={{0,1},{2,3},{4,5},{6,7},{8,9},{10,11},{12,13},{14,15},{16,17},{18,... | collective-permute-start | bytes 36872 | tf_op jit(solution)/shard_map/ppermute | solution.py:24
  124.9 3.1 %collective-permute-start.19 = (f32[2,6,1,256]{3,2,1,0:T(1,128)S(1)}, f32[2,6,1,256]{3,2,1,0:T(1,128)S(1)}, u32[]{:S(2)}, u32[]{:S(2)}) collective-permute-start(f32[2,6,1,256]{3,2,1,0:T(1,128)S(1)} %get-tuple-element.25), channel_id=1, source_target_pairs={{1,0},{3,2},{5,4},{7,6},{9,8},{11,10},{13,12},{15,14},{17,16},{19,... | collective-permute-start | bytes 36872 | tf_op jit(solution)/shard_map/ppermute | solution.py:26
  130.3 8.1 %collective-permute-start.20 = (f32[2,1,128,256]{3,2,1,0:T(8,128)S(1)}, f32[2,1,128,256]{3,2,1,0:T(8,128)S(1)}, u32[]{:S(2)}, u32[]{:S(2)}) collective-permute-start(f32[2,1,128,256]{3,2,1,0:T(8,128)S(1)} %get-tuple-element.36), channel_id=1, source_target_pairs={{0,4},{4,8},{8,12},{1,5},{5,9},{9,13},{2,6},{6,10},{10,14},{3,7},{... | collective-permute-start | bytes 786440 | tf_op jit(solution)/shard_map/ppermute | solution.py:24
  132.5 10.0 %collective-permute-start.21 = (f32[2,1,128,256]{3,2,1,0:T(8,128)S(1)}, f32[2,1,128,256]{3,2,1,0:T(8,128)S(1)}, u32[]{:S(2)}, u32[]{:S(2)}) collective-permute-start(f32[2,1,128,256]{3,2,1,0:T(8,128)S(1)} %get-tuple-element.37), channel_id=1, source_target_pairs={{4,0},{8,4},{12,8},{5,1},{9,5},{13,9},{6,2},{10,6},{14,10},{7,3},{... | collective-permute-start | bytes 786440 | tf_op jit(solution)/shard_map/ppermute | solution.py:26
  142.5 2.6 %collective-permute-start.22 = (f32[2,6,1,256]{3,2,1,0:T(1,128)S(1)}, f32[2,6,1,256]{3,2,1,0:T(1,128)S(1)}, u32[]{:S(2)}, u32[]{:S(2)}) collective-permute-start(f32[2,6,1,256]{3,2,1,0:T(1,128)S(1)} %get-tuple-element.22), channel_id=1, source_target_pairs={{0,1},{2,3},{4,5},{6,7},{8,9},{10,11},{12,13},{14,15},{16,17},{18,... | collective-permute-start | bytes 36872 | tf_op jit(solution)/shard_map/ppermute | solution.py:24
  143.8 3.1 %collective-permute-start.23 = (f32[2,6,1,256]{3,2,1,0:T(1,128)S(1)}, f32[2,6,1,256]{3,2,1,0:T(1,128)S(1)}, u32[]{:S(2)}, u32[]{:S(2)}) collective-permute-start(f32[2,6,1,256]{3,2,1,0:T(1,128)S(1)} %get-tuple-element.23), channel_id=1, source_target_pairs={{1,0},{3,2},{5,4},{7,6},{9,8},{11,10},{13,12},{15,14},{17,16},{19,... | collective-permute-start | bytes 36872 | tf_op jit(solution)/shard_map/ppermute | solution.py:26
  149.0 17.4 %copy-start.1 = (f32[2,4,128,256]{3,2,1,0:T(8,128)}, f32[2,4,128,256]{3,2,1,0:T(8,128)S(1)}, u32[]{:S(2)}) copy-start(f32[2,4,128,256]{3,2,1,0:T(8,128)S(1)} %fusion.44) | copy-start | bytes 3145732
  149.1 8.1 %collective-permute-start.24 = (f32[2,1,128,256]{3,2,1,0:T(8,128)S(1)}, f32[2,1,128,256]{3,2,1,0:T(8,128)S(1)}, u32[]{:S(2)}, u32[]{:S(2)}) collective-permute-start(f32[2,1,128,256]{3,2,1,0:T(8,128)S(1)} %get-tuple-element.34), channel_id=1, source_target_pairs={{0,4},{4,8},{8,12},{1,5},{5,9},{9,13},{2,6},{6,10},{10,14},{3,7},{... | collective-permute-start | bytes 786440 | tf_op jit(solution)/shard_map/ppermute | solution.py:24
  151.3 10.0 %collective-permute-start.25 = (f32[2,1,128,256]{3,2,1,0:T(8,128)S(1)}, f32[2,1,128,256]{3,2,1,0:T(8,128)S(1)}, u32[]{:S(2)}, u32[]{:S(2)}) collective-permute-start(f32[2,1,128,256]{3,2,1,0:T(8,128)S(1)} %get-tuple-element.35), channel_id=1, source_target_pairs={{4,0},{8,4},{12,8},{5,1},{9,5},{13,9},{6,2},{10,6},{14,10},{7,3},{... | collective-permute-start | bytes 786440 | tf_op jit(solution)/shard_map/ppermute | solution.py:26
  161.3 3.5 %collective-permute-start.26 = (f32[2,6,1,256]{3,2,1,0:T(1,128)S(1)}, f32[2,6,1,256]{3,2,1,0:T(1,128)S(1)}, u32[]{:S(2)}, u32[]{:S(2)}) collective-permute-start(f32[2,6,1,256]{3,2,1,0:T(1,128)S(1)} %get-tuple-element.20), channel_id=1, source_target_pairs={{0,1},{2,3},{4,5},{6,7},{8,9},{10,11},{12,13},{14,15},{16,17},{18,... | collective-permute-start | bytes 36872 | tf_op jit(solution)/shard_map/ppermute | solution.py:24
  162.6 3.1 %collective-permute-start.27 = (f32[2,6,1,256]{3,2,1,0:T(1,128)S(1)}, f32[2,6,1,256]{3,2,1,0:T(1,128)S(1)}, u32[]{:S(2)}, u32[]{:S(2)}) collective-permute-start(f32[2,6,1,256]{3,2,1,0:T(1,128)S(1)} %get-tuple-element.21), channel_id=1, source_target_pairs={{1,0},{3,2},{5,4},{7,6},{9,8},{11,10},{13,12},{15,14},{17,16},{19,... | collective-permute-start | bytes 36872 | tf_op jit(solution)/shard_map/ppermute | solution.py:26
  166.2 1.0 copy-start.4
Sparse Core Ops, SparseCore 0:
  171.8 12.7 reduce-scatter.1
where the time goes:
time: 192 us; the launch traced here: 191 us
  waiting for transfers between devices  92 us (48%)
  starting transfers between devices  46.8 us (24%)
  other arithmetic  25.5 us (13%)
  between operations  14.6 us (8%)
  blocking collectives  10.2 us (5%)
  local copies, waits for them, and re-layouts  2.36 us (1%)
    ppermute x14, waiting for transfers between devices, with_halo(): lax.ppermute(head, axis, [((i + 1) % count, i) for i in range(ends)])  41 us
    ppermute x14, waiting for transfers between devices, with_halo(): lax.ppermute(tail, axis, [(i, (i + 1) % count) for i in range(ends)])  38.1 us
    ppermute x14, starting transfers between devices, with_halo(): lax.ppermute(tail, axis, [(i, (i + 1) % count) for i in range(ends)])  28.5 us
    ppermute x14, starting transfers between devices, with_halo(): lax.ppermute(head, axis, [((i + 1) % count, i) for i in range(ends)])  18.3 us
    reduce_scatter x1, waiting for transfers between devices, body(): lax.psum_scatter(local_term, 'section', scatter_dimension=2, tiled=True)  12.9 us
    add x5, other arithmetic, body(): adjoint_field = crop(adjoint_field, field_depth, field_depth - 1) + update  10.9 us
    all_gather x1, blocking collectives, body(): lax.all_gather(material_share, 'section', axis=2, tiled=True)  10.2 us
  transfers between devices with their start and end apart: 29, of which 22 were waited for; matrix products, arithmetic and copies ran while one was open for 1% of the time, Pallas kernels for 0%

commit v1 on v0

v1 whole, which is shorter than its diff:
```python
import functools

import jax
import jax.numpy as jnp
from jax import lax
from jax.experimental import pallas as pl
from jax.experimental.pallas import tpu as pltpu
from jax.sharding import PartitionSpec as P

SWEEPS = 6
LOSS_RATE = 0.05
FLOOR_COND = 0.001
SIMP_POWER = 3.0
BOUND_LOW = 0.05
BOUND_HIGH = 2.0
CENTER = 0.5 * (BOUND_HIGH + BOUND_LOW)
HALF_WIDTH = 0.5 * (BOUND_HIGH - BOUND_LOW)
MESH = pl.DeviceIdType.MESH
PAD = 8


def factors():
    ratio = CENTER / HALF_WIDTH
    factor = 1.0 / ratio
    table = []
    for _ in range(1, SWEEPS):
        factor_next = 1.0 / (2.0 * ratio - factor)
        table.append((factor_next * factor, 2.0 * factor_next / HALF_WIDTH))
        factor = factor_next
    return table


def pick(index, values):
    out = jnp.float32(values[0])
    for i in range(1, len(values)):
        out = jnp.where(index == i, jnp.float32(values[i]), out)
    return out


def kernel(
    sizes,
    m_ref, t_ref, g_ref, depth_ref, layer_ref,
    adj_ref, sens_ref,
    field, temp, grad, update, inverse, cond, share,
    cxl, cxr, cyu, cyd, cz, part_out, part_in,
    load_sem, store_sem,
    mx_send, mx_recv, mz_send, mz_recv, my_send, my_recv,
    tz_send, tz_recv, ty_send, ty_recv,
    vz_send, vz_recv, vy_send, vy_recv,
    ex_send, ex_recv,
):
    nz, nx, ny, total_planes = sizes
    sections, planes, rows, cols = t_ref.shape
    width = m_ref.shape[2]
    lo, hi = PAD, PAD + rows
    me_z, me_x, me_y = lax.axis_index("slab"), lax.axis_index("section"), lax.axis_index("col")
    body = pl.ds(lo, rows)
    chunk = min(32, rows)
    starts = list(range(0, rows, chunk))

    def xpeer(k):
        return lax.rem(me_x + k, nx)

    zsides = (("slab", me_z > 0, me_z - 1), ("slab", me_z < nz - 1, me_z + 1))
    ysides = (("col", me_y > 0, me_y - 1), ("col", me_y < ny - 1, me_y + 1))

    barrier = pltpu.get_barrier_semaphore()
    count = jnp.int32(nx - 1)
    for k in range(1, nx):
        pl.semaphore_signal(barrier, inc=1, device_id={"section": xpeer(k)}, device_id_type=MESH)
    for name, has, index in zsides + ysides:
        count = count + jnp.where(has, nx, 0)

        @pl.when(has)
        def _():
            for k in range(nx):
                pl.semaphore_signal(
                    barrier, inc=1, device_id={name: index, "section": xpeer(k)}, device_id_type=MESH
                )

    load_m = pltpu.make_async_copy(m_ref, share.at[me_x, pl.ds(1, planes), body], load_sem.at[0])
    load_t = pltpu.make_async_copy(t_ref, temp.at[:, pl.ds(1, planes), body], load_sem.at[1])
    load_g = pltpu.make_async_copy(g_ref, grad, load_sem.at[2])
    load_m.start()
    load_t.start()
    load_g.start()

    for side, (name, has, index) in enumerate(zsides):
        plane = 0 if side == 0 else planes + 1

        @pl.when(jnp.logical_not(has))
        def _():
            for s in range(sections):
                for par in range(2):
                    field[par, s, plane] = jnp.zeros((rows + 2 * PAD, cols), jnp.float32)
                temp[s, plane] = jnp.zeros((rows + 2 * PAD, cols), jnp.float32)
            for k in range(nx):
                share[k, plane] = jnp.zeros((rows + 2 * PAD, width), jnp.float32)

    for side, (name, has, index) in enumerate(ysides):
        first = 0 if side == 0 else hi

        @pl.when(jnp.logical_not(has))
        def _():
            for p in range(1, planes + 1):
                for s in range(sections):
                    for par in range(2):
                        field[par, s, p, first : first + PAD] = jnp.zeros((PAD, cols), jnp.float32)
                    temp[s, p, first : first + PAD] = jnp.zeros((PAD, cols), jnp.float32)
                for k in range(nx):
                    share[k, p, first : first + PAD] = jnp.zeros((PAD, width), jnp.float32)

    pl.semaphore_wait(barrier, count)

    def remote(src, dst, send, recv, device):
        return pltpu.make_async_remote_copy(
            src_ref=src, dst_ref=dst, send_sem=send, recv_sem=recv, device_id=device, device_id_type=MESH
        )

    def mx_copy(k, slot):
        return remote(
            m_ref, share.at[slot, pl.ds(1, planes), body], mx_send.at[k], mx_recv.at[slot],
            {"section": xpeer(k)},
        )

    def mz_copy(side, k, slot):
        src = m_ref.at[0 if side == 0 else planes - 1]
        dst = share.at[slot, planes + 1 if side == 0 else 0, body]
        return remote(
            src, dst, mz_send.at[side, k], mz_recv.at[side, slot],
            {"slab": zsides[side][2], "section": xpeer(k)},
        )

    def my_copy(side, k, slot):
        src = m_ref.at[:, pl.ds(0 if side == 0 else rows - PAD, PAD)]
        dst = share.at[slot, pl.ds(1, planes), pl.ds(hi if side == 0 else 0, PAD)]
        return remote(
            src, dst, my_send.at[side, k], my_recv.at[side, slot],
            {"col": ysides[side][2], "section": xpeer(k)},
        )

    def tz_copy(side):
        src = t_ref.at[:, 0 if side == 0 else planes - 1]
        dst = temp.at[:, planes + 1 if side == 0 else 0, body]
        return remote(src, dst, tz_send.at[side], tz_recv.at[side], {"slab": zsides[side][2]})

    def ty_copy(side):
        src = t_ref.at[:, :, pl.ds(0 if side == 0 else rows - PAD, PAD)]
        dst = temp.at[:, pl.ds(1, planes), pl.ds(hi if side == 0 else 0, PAD)]
        return remote(src, dst, ty_send.at[side], ty_recv.at[side], {"col": ysides[side][2]})

    def vz_copy(side, s, par):
        src = field.at[par, s, 1 if side == 0 else planes, body]
        dst = field.at[par, s, planes + 1 if side == 0 else 0, body]
        return remote(
            src, dst, vz_send.at[side, s, par], vz_recv.at[side, s, par], {"slab": zsides[side][2]}
        )

    spans = [(1, 1), (planes, 1), (2, planes - 2)]

    def vy_copy(side, s, group, par):
        first, number = spans[group]
        src = field.at[par, s, pl.ds(first, number), pl.ds(lo if side == 0 else hi - PAD, PAD)]
        dst = field.at[par, s, pl.ds(first, number), pl.ds(hi if side == 0 else 0, PAD)]
        return remote(
            src, dst, vy_send.at[side, s, group, par], vy_recv.at[side, s, group, par],
            {"col": ysides[side][2]},
        )

    def each(sides, action):
        for side, (name, has, index) in enumerate(sides):
            @pl.when(has)
            def _():
                action(side)

    for k in range(1, nx):
        mx_copy(k, me_x).start()
    each(ysides, lambda side: [my_copy(side, k, me_x).start() for k in range(nx)])
    each(zsides, lambda side: [mz_copy(side, k, me_x).start() for k in range(nx)])
    each(ysides, lambda side: ty_copy(side).start())
    each(zsides, lambda side: tz_copy(side).start())

    def live(s, p):
        plane = me_z * planes - 1 + p
        inside = (plane >= 0) & (plane < total_planes)
        layer = layer_ref[jnp.clip(plane, 0, total_planes - 1)]
        return jnp.where(inside & (layer < depth_ref[s]), jnp.float32(1.0), jnp.float32(0.0))

    active = [[live(s, p) for p in range(planes + 2)] for s in range(sections)]

    load_m.wait()
    for k in range(1, nx):
        mx_copy(k, xpeer(k)).wait_recv()
    each(ysides, lambda side: [my_copy(1 - side, k, k).wait_recv() for k in range(nx)])
    each(zsides, lambda side: [mz_copy(1 - side, k, k).wait_recv() for k in range(nx)])

    def conduct_block(p, r0, number):
        whole = jnp.concatenate([share[k, p, pl.ds(r0, number)] for k in range(nx)], axis=-1)
        cond[p, pl.ds(r0, number)] = 0.5 * (
            FLOOR_COND + (1.0 - FLOOR_COND) * (whole * whole * whole)
        )

    def conduct_plane(p, _):
        for r0 in range(0, rows + 2 * PAD, PAD * 2):
            conduct_block(p, r0, PAD * 2)
        return 0

    lax.fori_loop(1, planes + 1, conduct_plane, 0)
    for p in (0, planes + 1):
        for r0 in starts:
            conduct_block(p, lo + r0, chunk)

    lane = lax.broadcasted_iota(jnp.int32, (chunk, cols), 1)
    row = lax.broadcasted_iota(jnp.int32, (chunk, cols), 0)
    up_mask = jnp.where((row == 0) & (me_y == 0), jnp.float32(0.0), jnp.float32(1.0))
    down_mask = jnp.where((row == chunk - 1) & (me_y == ny - 1), jnp.float32(0.0), jnp.float32(1.0))

    def left(x):
        return pltpu.roll(x, 1, 1)

    def right(x):
        return pltpu.roll(x, cols - 1, 1)

    load_g.wait()

    def setup_chunk(p, r0, act):
        at = pl.ds(r0, chunk)
        h = cond[p, pl.ds(lo + r0, chunk)]
        xl = jnp.where(lane == 0, 0.0, h + left(h))
        xr = jnp.where(lane == cols - 1, 0.0, h + right(h))
        yu = h + cond[p, pl.ds(lo + r0 - 1, chunk)]
        yd = h + cond[p, pl.ds(lo + r0 + 1, chunk)]
        if r0 == 0:
            yu = yu * up_mask
        if r0 == rows - chunk:
            yd = yd * down_mask
        zu = h + cond[p - 1, pl.ds(lo + r0, chunk)]
        zd = h + cond[p + 1, pl.ds(lo + r0, chunk)]
        cxl[p - 1, at] = xl
        cxr[p - 1, at] = xr
        cyu[p - 1, at] = yu
        cyd[p - 1, at] = yd
        cz[p - 1, at] = zu
        cz[p, at] = zd
        flat = (xl + xr) + (yu + yd)
        for s in range(sections):
            above, here, below = act[s]
            diagonal = (LOSS_RATE * here + (1.0 - here)) + here * (flat + above * zu + below * zd)
            inv = here / diagonal
            g = inv * grad[s, p - 1, at]
            inverse[s, p - 1, at] = inv
            grad[s, p - 1, at] = g
            first = g * (1.0 / CENTER)
            update[s, p - 1, at] = first
            field[1, s, p, pl.ds(lo + r0, chunk)] = first

    def start_edges(s, par):
        each(zsides, lambda side: vz_copy(side, s, par).start())
        each(ysides, lambda side: [vy_copy(side, s, group, par).start() for group in (0, 1)])

    def start_inner(s, par):
        if planes > 2:
            each(ysides, lambda side: vy_copy(side, s, 2, par).start())

    def setup_plane(p):
        act = [active[s][p - 1 : p + 2] for s in range(sections)]
        for r0 in starts:
            setup_chunk(p, r0, act)

    setup_plane(1)
    setup_plane(planes)
    for s in range(sections):
        start_edges(s, 1)
    for p in range(2, planes):
        setup_plane(p)
    for s in range(sections):
        start_inner(s, 1)

    table = factors()

    def relax_plane(s, p, now, new, alpha, beta):
        for r0 in starts:
            at = pl.ds(r0, chunk)
            v = field[now, s, p, pl.ds(lo + r0, chunk)]
            total = cxl[p - 1, at] * left(v) + cxr[p - 1, at] * right(v)
            total += cyu[p - 1, at] * field[now, s, p, pl.ds(lo + r0 - 1, chunk)]
            total += cyd[p - 1, at] * field[now, s, p, pl.ds(lo + r0 + 1, chunk)]
            total += cz[p - 1, at] * field[now, s, p - 1, pl.ds(lo + r0, chunk)]
            total += cz[p, at] * field[now, s, p + 1, pl.ds(lo + r0, chunk)]
            u = alpha * update[s, p - 1, at] + beta * (
                (grad[s, p - 1, at] - v) + inverse[s, p - 1, at] * total
            )
            update[s, p - 1, at] = u
            field[new, s, p, pl.ds(lo + r0, chunk)] = v + u

    def sweep(n, _):
        now, new = lax.rem(n - 1, 2), lax.rem(n, 2)
        alpha = pick(n - 2, [a for a, _ in table])
        beta = pick(n - 2, [b for _, b in table])
        for s in range(sections):
            each(zsides, lambda side: vz_copy(1 - side, s, now).wait_recv())
            each(ysides, lambda side: [vy_copy(1 - side, s, group, now).wait_recv() for group in (0, 1)])

            def edge(i, _):
                relax_plane(s, 1 + i * (planes - 1), now, new, alpha, beta)
                return 0

            lax.fori_loop(0, 2, edge, 0)
            start_edges(s, new)
            if planes > 2:
                each(ysides, lambda side: vy_copy(1 - side, s, 2, now).wait_recv())

                def inner(p, _):
                    relax_plane(s, p, now, new, alpha, beta)
                    return 0

                lax.fori_loop(2, planes, inner, 0)
                start_inner(s, new)
                each(ysides, lambda side: vy_copy(side, s, 2, now).wait_send())
            each(zsides, lambda side: vz_copy(side, s, now).wait_send())
            each(ysides, lambda side: [vy_copy(side, s, group, now).wait_send() for group in (0, 1)])
        return 0

    lax.fori_loop(2, SWEEPS + 1, sweep, 0)

    last = SWEEPS % 2
    store = pltpu.make_async_copy(field.at[last, :, pl.ds(1, planes), body], adj_ref, store_sem)
    store.start()

    def ex_copy(k, p, slot):
        return remote(
            part_out.at[slot[0], p - 1], part_in.at[slot[1], p - 1], ex_send.at[k, p - 1],
            ex_recv.at[slot[1], p - 1], {"section": xpeer(k)},
        )

    def energy_plane(p):
        for r0 in starts:
            rest = jnp.zeros((chunk, cols), jnp.float32)
            across = jnp.zeros((chunk, cols), jnp.float32)
            for s in range(sections):
                above, here, below = active[s][p - 1 : p + 2]

                def both(plane, shift):
                    at = pl.ds(lo + r0 + shift, chunk)
                    return field[last, s, plane, at], temp[s, plane, at]

                v, t = both(p, 0)
                across += here * ((v - left(v)) * (t - left(t)))
                v2, t2 = both(p, -1)
                term = (v - v2) * (t - t2)
                if r0 == 0:
                    term = term * up_mask
                v2, t2 = both(p, 1)
                more = (v - v2) * (t - t2)
                if r0 == rows - chunk:
                    more = more * down_mask
                term += more
                v2, t2 = both(p - 1, 0)
                term += above * ((v - v2) * (t - t2))
                v2, t2 = both(p + 1, 0)
                term += below * ((v - v2) * (t - t2))
                rest += here * term
            across = jnp.where(lane == 0, 0.0, across)
            total = 0.5 * (rest + (across + right(across)))
            for k in range(nx):
                part_out[k, p - 1, pl.ds(r0, chunk)] = total[:, k * width : (k + 1) * width]
        for k in range(1, nx):
            ex_copy(k, p, (xpeer(k), me_x)).start()

    each(ysides, lambda side: ty_copy(1 - side).wait_recv())
    load_t.wait()
    for s in range(sections):
        each(ysides, lambda side: [vy_copy(1 - side, s, g, last).wait_recv() for g in (0, 1)])
        if planes > 2:
            each(ysides, lambda side: vy_copy(1 - side, s, 2, last).wait_recv())
    for p in range(2, planes):
        energy_plane(p)
    each(zsides, lambda side: tz_copy(1 - side).wait_recv())
    for s in range(sections):
        each(zsides, lambda side: vz_copy(1 - side, s, last).wait_recv())
    energy_plane(1)
    energy_plane(planes)

    for p in list(range(2, planes)) + [1, planes]:
        for k in range(1, nx):
            ex_copy(k, p, (xpeer(k), xpeer(k))).wait_recv()
        for r0 in starts:
            at = pl.ds(r0, chunk)
            total = part_out[me_x, p - 1, at]
            for k in range(1, nx):
                total += part_in[xpeer(k), p - 1, at]
            m = share[me_x, p, pl.ds(lo + r0, chunk)]
            sens_ref[p - 1, at] = (-(1.0 - FLOOR_COND) * SIMP_POWER) * (m * m) * total

    for k in range(1, nx):
        mx_copy(k, me_x).wait_send()
        for p in range(1, planes + 1):
            ex_copy(k, p, (xpeer(k), me_x)).wait_send()
    each(ysides, lambda side: [my_copy(side, k, me_x).wait_send() for k in range(nx)])
    each(zsides, lambda side: [mz_copy(side, k, me_x).wait_send() for k in range(nx)])
    each(ysides, lambda side: ty_copy(side).wait_send())
    each(zsides, lambda side: tz_copy(side).wait_send())
    for s in range(sections):
        each(zsides, lambda side: vz_copy(side, s, last).wait_send())
        each(ysides, lambda side: [vy_copy(side, s, g, last).wait_send() for g in (0, 1)])
        if planes > 2:
            each(ysides, lambda side: vy_copy(side, s, 2, last).wait_send())
    store.wait()


def solution(mesh):
    nz, nx, ny = mesh.shape["slab"], mesh.shape["section"], mesh.shape["col"]

    def body(material_share, stored_thermal_state, objective_slope, print_depths, slice_to_deposit):
        sections, planes, rows, cols = stored_thermal_state.shape
        width = material_share.shape[2]
        f32 = jnp.float32
        tall = rows + 2 * PAD
        dma = pltpu.SemaphoreType.DMA
        inner = (planes, rows, cols)
        anywhere = pl.BlockSpec(memory_space=pl.ANY)
        return pl.pallas_call(
            functools.partial(kernel, (nz, nx, ny, slice_to_deposit.shape[0])),
            out_shape=(
                jax.ShapeDtypeStruct(stored_thermal_state.shape, f32),
                jax.ShapeDtypeStruct(material_share.shape, f32),
            ),
            in_specs=[anywhere] * 3 + [pl.BlockSpec(memory_space=pltpu.SMEM)] * 2,
            out_specs=(anywhere, pl.BlockSpec(memory_space=pltpu.VMEM)),
            scratch_shapes=[
                pltpu.VMEM((2, sections, planes + 2, tall, cols), f32),
                pltpu.VMEM((sections, planes + 2, tall, cols), f32),
                pltpu.VMEM((sections,) + inner, f32),
                pltpu.VMEM((sections,) + inner, f32),
                pltpu.VMEM((sections,) + inner, f32),
                pltpu.VMEM((planes + 2, tall, cols), f32),
                pltpu.VMEM((nx, planes + 2, tall, width), f32),
                pltpu.VMEM(inner, f32),
                pltpu.VMEM(inner, f32),
                pltpu.VMEM(inner, f32),
                pltpu.VMEM(inner, f32),
                pltpu.VMEM((planes + 1, rows, cols), f32),
                pltpu.VMEM((nx, planes, rows, width), f32),
                pltpu.VMEM((nx, planes, rows, width), f32),
                dma((3,)),
                dma(()),
                dma((nx,)), dma((nx,)),
                dma((2, nx)), dma((2, nx)),
                dma((2, nx)), dma((2, nx)),
                dma((2,)), dma((2,)),
                dma((2,)), dma((2,)),
                dma((2, sections, 2)), dma((2, sections, 2)),
                dma((2, sections, 3, 2)), dma((2, sections, 3, 2)),
                dma((nx, planes)), dma((nx, planes)),
            ],
            compiler_params=pltpu.CompilerParams(
                collective_id=0, has_side_effects=True, vmem_limit_bytes=40 * 1024 * 1024
            ),
        )(material_share, stored_thermal_state, objective_slope, print_depths, slice_to_deposit)

    return jax.shard_map(
        body,
        mesh=mesh,
        in_specs=(
            P(("parts", "slab"), "col", "section"),
            P(("parts", "section"), "slab", "col", None),
            P(("parts", "section"), "slab", "col", None),
            P(("parts", "section")),
            P("parts"),
        ),
        out_specs=(
            P(("parts", "section"), "slab", "col", None),
            P(("parts", "slab"), "col", "section"),
        ),
        check_vma=False,
    )
```

time: 192 us -> 64.8 us (0.34)
  waiting for transfers between devices: 92 us -> 0 us
  Pallas kernels: 0 us -> 57.5 us
  starting transfers between devices: 46.8 us -> 0 us
  other arithmetic: 25.5 us -> 0 us
  between operations: 14.6 us -> 0.65 us
  blocking collectives: 10.2 us -> 0 us
  local copies, waits for them, and re-layouts: 2.36 us -> 6.38 us
    ppermute x28 -> x0, waiting for transfers between devices: 79.1 us -> none  [the longest x14 41 us: with_halo(): lax.ppermute(head, axis, [((i + 1) % count, i) for i in range(ends)])]
    pallas_call x0 -> x1, Pallas kernels: none -> 57.5 us  [body(): pl.pallas_call(functools.partial(kernel, (nz, nx, ny, slice_to_deposit.sh...]
    ppermute x28 -> x0, starting transfers between devices: 46.8 us -> none  [the longest x14 28.5 us: with_halo(): lax.ppermute(tail, axis, [(i, (i + 1) % count) for i in range(ends)])]
    reduce_scatter x1 -> x0, waiting for transfers between devices: 12.9 us -> none  [body(): lax.psum_scatter(local_term, 'section', scatter_dimension=2, tiled=True)]
    add x11 -> x0, other arithmetic: 12.5 us -> none  [the longest x5 10.9 us: body(): adjoint_field = crop(adjoint_field, field_depth, field_depth - 1) + update]
    all_gather x1 -> x0, blocking collectives: 10.2 us -> none  [body(): lax.all_gather(material_share, 'section', axis=2, tiled=True)]
    mul x10 -> x0, other arithmetic: 5.62 us -> none  [the longest x1 2.71 us: face_energy(): 0.5 * active_wide[:, :, 1:] * active_wide[:, :, :-1]]
    unnamed x14 -> x12, local copies, waits for them, and re-layouts: 0.85 us -> 6.38 us
  transfers between devices with their start and end apart: 29 -> 0, of which waited for: 22 -> 0; matrix products, arithmetic and copies ran while one was open for 1% -> 0% of each run, Pallas kernels for 0% -> 0%
where the time goes in v1:
time: 64.8 us; the launch traced here: 64.6 us
  Pallas kernels  57.5 us (89%)
  local copies, waits for them, and re-layouts  6.38 us (10%)
  between operations  0.65 us (1%)
    pallas_call x1, Pallas kernels, body(): pl.pallas_call(functools.partial(kernel, (nz, nx, ny, slice_to_deposit.sh...  57.5 us
    unnamed x12, local copies, waits for them, and re-layouts  6.38 us

profile of v1, /device:TPU:0, one launch (start us, length us, event | category | flops | bytes accessed | tf_op | source)
XLA Modules:
  0.0 64.6 jit_solution(458839899261039947)
XLA Ops:
  0.6 0.0 copy-start
  0.6 1.2 %copy-done = f32[2,4,128,256]{3,2,1,0:T(8,128)S(1)} copy-done((f32[2,4,128,256]{3,2,1,0:T(8,128)S(1)}, f32[2,4,128,256]{3,2,1,0:T(8,128)}, u32[]{:S(2)}) %copy-start) | copy-done | bytes 1048600
  1.9 0.0 copy-start.1
  1.9 1.2 %copy-done.1 = f32[2,4,128,256]{3,2,1,0:T(8,128)S(1)} copy-done((f32[2,4,128,256]{3,2,1,0:T(8,128)S(1)}, f32[2,4,128,256]{3,2,1,0:T(8,128)}, u32[]{:S(2)}) %copy-start.1) | copy-done | bytes 1048600
  3.1 0.0 copy-start.2
  3.1 0.9 %copy-done.2 = f32[4,128,128]{2,1,0:T(8,128)S(1)} copy-done((f32[4,128,128]{2,1,0:T(8,128)S(1)}, f32[4,128,128]{2,1,0:T(8,128)}, u32[]{:S(2)}) %copy-start.2) | copy-done | bytes 262168
  4.0 0.0 copy-start.3
  4.0 0.7 %copy-done.3 = s32[2]{0:T(128)S(1)} copy-done((s32[2]{0:T(128)S(1)}, s32[2]{0:T(128)}, u32[]{:S(2)}) %copy-start.3) | copy-done | bytes 32
  4.7 0.0 copy-start.4
  4.7 0.7 %copy-done.4 = s32[16]{0:T(128)S(1)} copy-done((s32[16]{0:T(128)S(1)}, s32[16]{0:T(128)}, u32[]{:S(2)}) %copy-start.4) | copy-done | bytes 88
  5.3 57.5 %shard_map.68 = (f32[2,4,128,256]{3,2,1,0:T(8,128)S(1)}, f32[4,128,128]{2,1,0:T(8,128)S(1)}) custom-call(f32[4,128,128]{2,1,0:T(8,128)S(1)} %copy-done.2, f32[2,4,128,256]{3,2,1,0:T(8,128)S(1)} %copy-done, f32[2,4,128,256]{3,2,1,0:T(8,128)S(1)} %copy-done.1, s32[2]{0:T(128)S(1)} %copy-done.3, s32[16]{0:T(128)S(1)} %copy-done.4), custom_call_target="tpu_custom_call" | custom-call | tf_op jit(solution)/shard_map/pallas_call | solution.py:422
  62.9 1.0 %copy.9 = f32[2,4,128,256]{3,2,1,0:T(8,128)} copy(f32[2,4,128,256]{3,2,1,0:T(8,128)S(1)} %get-tuple-element.4) | data formatting | bytes 2097152
  63.9 0.7 %copy.10 = f32[4,128,128]{2,1,0:T(8,128)} copy(f32[4,128,128]{2,1,0:T(8,128)S(1)} %get-tuple-element.5) | data formatting | bytes 524288
Async XLA Ops:
  0.6 1.2 %copy-start = (f32[2,4,128,256]{3,2,1,0:T(8,128)S(1)}, f32[2,4,128,256]{3,2,1,0:T(8,128)}, u32[]{:S(2)}) copy-start(f32[2,4,128,256]{3,2,1,0:T(8,128)} %t_ref.1) | copy-start | bytes 3145732
  1.9 1.2 %copy-start.1 = (f32[2,4,128,256]{3,2,1,0:T(8,128)S(1)}, f32[2,4,128,256]{3,2,1,0:T(8,128)}, u32[]{:S(2)}) copy-start(f32[2,4,128,256]{3,2,1,0:T(8,128)} %g_ref.1) | copy-start | bytes 3145732
  3.1 0.9 %copy-start.2 = (f32[4,128,128]{2,1,0:T(8,128)S(1)}, f32[4,128,128]{2,1,0:T(8,128)}, u32[]{:S(2)}) copy-start(f32[4,128,128]{2,1,0:T(8,128)} %m_ref.1) | copy-start | bytes 786436
  4.0 0.7 %copy-start.3 = (s32[2]{0:T(128)S(1)}, s32[2]{0:T(128)}, u32[]{:S(2)}) copy-start(s32[2]{0:T(128)} %depth_ref.1) | copy-start | bytes 28
  4.7 0.7 %copy-start.4 = (s32[16]{0:T(128)S(1)}, s32[16]{0:T(128)}, u32[]{:S(2)}) copy-start(s32[16]{0:T(128)} %layer_ref.1) | copy-start | bytes 196

commit v2 on v1

--- a/solution.py
+++ b/solution.py
@@ -30,18 +30,11 @@
     return table
 
 
-def pick(index, values):
-    out = jnp.float32(values[0])
-    for i in range(1, len(values)):
-        out = jnp.where(index == i, jnp.float32(values[i]), out)
-    return out
-
-
 def kernel(
     sizes,
     m_ref, t_ref, g_ref, depth_ref, layer_ref,
     adj_ref, sens_ref,
-    field, temp, grad, update, inverse, cond, share,
+    even, odd, temp, grad, update, inverse, cond, share,
     cxl, cxr, cyu, cyd, cz, part_out, part_in,
     load_sem, store_sem,
     mx_send, mx_recv, mz_send, mz_recv, my_send, my_recv,
@@ -52,6 +45,10 @@
     nz, nx, ny, total_planes = sizes
     sections, planes, rows, cols = t_ref.shape
     width = m_ref.shape[2]
+    fields = (even, odd)
+    lanes = even.shape[-1]
+    parts = cols // lanes
+    halves = range(parts)
     lo, hi = PAD, PAD + rows
     me_z, me_x, me_y = lax.axis_index("slab"), lax.axis_index("section"), lax.axis_index("col")
     body = pl.ds(lo, rows)
@@ -79,11 +76,21 @@
                 )
 
     load_m = pltpu.make_async_copy(m_ref, share.at[me_x, pl.ds(1, planes), body], load_sem.at[0])
-    load_t = pltpu.make_async_copy(t_ref, temp.at[:, pl.ds(1, planes), body], load_sem.at[1])
-    load_g = pltpu.make_async_copy(g_ref, grad, load_sem.at[2])
-    load_m.start()
-    load_t.start()
-    load_g.start()
+    load_t = [
+        pltpu.make_async_copy(
+            t_ref.at[:, :, :, pl.ds(h * lanes, lanes)], temp.at[:, pl.ds(1, planes), h, body],
+            load_sem.at[1 + h],
+        )
+        for h in halves
+    ]
+    load_g = [
+        pltpu.make_async_copy(
+            g_ref.at[:, :, :, pl.ds(h * lanes, lanes)], grad.at[:, :, h], load_sem.at[1 + parts + h]
+        )
+        for h in halves
+    ]
+    for load in [load_m] + load_t + load_g:
+        load.start()
 
     for side, (name, has, index) in enumerate(zsides):
         plane = 0 if side == 0 else planes + 1
@@ -92,8 +99,8 @@
         def _():
             for s in range(sections):
                 for par in range(2):
-                    field[par, s, plane] = jnp.zeros((rows + 2 * PAD, cols), jnp.float32)
-                temp[s, plane] = jnp.zeros((rows + 2 * PAD, cols), jnp.float32)
+                    fields[par][s, plane] = jnp.zeros(even.shape[2:], jnp.float32)
+                temp[s, plane] = jnp.zeros(temp.shape[2:], jnp.float32)
             for k in range(nx):
                 share[k, plane] = jnp.zeros((rows + 2 * PAD, width), jnp.float32)
 
@@ -105,8 +112,8 @@
             for p in range(1, planes + 1):
                 for s in range(sections):
                     for par in range(2):
-                        field[par, s, p, first : first + PAD] = jnp.zeros((PAD, cols), jnp.float32)
-                    temp[s, p, first : first + PAD] = jnp.zeros((PAD, cols), jnp.float32)
+                        fields[par][s, p, :, first : first + PAD] = jnp.zeros((parts, PAD, lanes), jnp.float32)
+                    temp[s, p, :, first : first + PAD] = jnp.zeros((parts, PAD, lanes), jnp.float32)
                 for k in range(nx):
                     share[k, p, first : first + PAD] = jnp.zeros((PAD, width), jnp.float32)
 
@@ -140,18 +147,18 @@
         )
 
     def tz_copy(side):
-        src = t_ref.at[:, 0 if side == 0 else planes - 1]
-        dst = temp.at[:, planes + 1 if side == 0 else 0, body]
+        src = temp.at[:, 1 if side == 0 else planes, :, body]
+        dst = temp.at[:, planes + 1 if side == 0 else 0, :, body]
         return remote(src, dst, tz_send.at[side], tz_recv.at[side], {"slab": zsides[side][2]})
 
     def ty_copy(side):
-        src = t_ref.at[:, :, pl.ds(0 if side == 0 else rows - PAD, PAD)]
-        dst = temp.at[:, pl.ds(1, planes), pl.ds(hi if side == 0 else 0, PAD)]
+        src = temp.at[:, pl.ds(1, planes), :, pl.ds(lo if side == 0 else hi - PAD, PAD)]
+        dst = temp.at[:, pl.ds(1, planes), :, pl.ds(hi if side == 0 else 0, PAD)]
         return remote(src, dst, ty_send.at[side], ty_recv.at[side], {"col": ysides[side][2]})
 
     def vz_copy(side, s, par):
-        src = field.at[par, s, 1 if side == 0 else planes, body]
-        dst = field.at[par, s, planes + 1 if side == 0 else 0, body]
+        src = fields[par].at[s, 1 if side == 0 else planes, :, body]
+        dst = fields[par].at[s, planes + 1 if side == 0 else 0, :, body]
         return remote(
             src, dst, vz_send.at[side, s, par], vz_recv.at[side, s, par], {"slab": zsides[side][2]}
         )
@@ -160,8 +167,8 @@
 
     def vy_copy(side, s, group, par):
         first, number = spans[group]
-        src = field.at[par, s, pl.ds(first, number), pl.ds(lo if side == 0 else hi - PAD, PAD)]
-        dst = field.at[par, s, pl.ds(first, number), pl.ds(hi if side == 0 else 0, PAD)]
+        src = fields[par].at[s, pl.ds(first, number), :, pl.ds(lo if side == 0 else hi - PAD, PAD)]
+        dst = fields[par].at[s, pl.ds(first, number), :, pl.ds(hi if side == 0 else 0, PAD)]
         return remote(
             src, dst, vy_send.at[side, s, group, par], vy_recv.at[side, s, group, par],
             {"col": ysides[side][2]},
@@ -177,6 +184,8 @@
         mx_copy(k, me_x).start()
     each(ysides, lambda side: [my_copy(side, k, me_x).start() for k in range(nx)])
     each(zsides, lambda side: [mz_copy(side, k, me_x).start() for k in range(nx)])
+    for load in load_t:
+        load.wait()
     each(ysides, lambda side: ty_copy(side).start())
     each(zsides, lambda side: tz_copy(side).start())
 
@@ -196,9 +205,9 @@
 
     def conduct_block(p, r0, number):
         whole = jnp.concatenate([share[k, p, pl.ds(r0, number)] for k in range(nx)], axis=-1)
-        cond[p, pl.ds(r0, number)] = 0.5 * (
-            FLOOR_COND + (1.0 - FLOOR_COND) * (whole * whole * whole)
-        )
+        whole = 0.5 * (FLOOR_COND + (1.0 - FLOOR_COND) * (whole * whole * whole))
+        for h in halves:
+            cond[p, h, pl.ds(r0, number)] = whole[:, h * lanes : (h + 1) * lanes]
 
     def conduct_plane(p, _):
         for r0 in range(0, rows + 2 * PAD, PAD * 2):
@@ -210,49 +219,63 @@
         for r0 in starts:
             conduct_block(p, lo + r0, chunk)
 
-    lane = lax.broadcasted_iota(jnp.int32, (chunk, cols), 1)
-    row = lax.broadcasted_iota(jnp.int32, (chunk, cols), 0)
+    lane = lax.broadcasted_iota(jnp.int32, (chunk, lanes), 1)
+    row = lax.broadcasted_iota(jnp.int32, (chunk, lanes), 0)
     up_mask = jnp.where((row == 0) & (me_y == 0), jnp.float32(0.0), jnp.float32(1.0))
     down_mask = jnp.where((row == chunk - 1) & (me_y == ny - 1), jnp.float32(0.0), jnp.float32(1.0))
 
-    def left(x):
-        return pltpu.roll(x, 1, 1)
-
-    def right(x):
-        return pltpu.roll(x, cols - 1, 1)
-
-    load_g.wait()
+    def left(xs):
+        turned = [pltpu.roll(x, 1, 1) for x in xs]
+        return [turned[0]] + [jnp.where(lane == 0, turned[h - 1], turned[h]) for h in halves[1:]]
+
+    def right(xs):
+        turned = [pltpu.roll(x, lanes - 1, 1) for x in xs]
+        return [
+            jnp.where(lane == lanes - 1, turned[h + 1], turned[h]) for h in halves[:-1]
+        ] + [turned[-1]]
+
+    for load in load_g:
+        load.wait()
 
     def setup_chunk(p, r0, act):
         at = pl.ds(r0, chunk)
-        h = cond[p, pl.ds(lo + r0, chunk)]
-        xl = jnp.where(lane == 0, 0.0, h + left(h))
-        xr = jnp.where(lane == cols - 1, 0.0, h + right(h))
-        yu = h + cond[p, pl.ds(lo + r0 - 1, chunk)]
-        yd = h + cond[p, pl.ds(lo + r0 + 1, chunk)]
-        if r0 == 0:
-            yu = yu * up_mask
-        if r0 == rows - chunk:
-            yd = yd * down_mask
-        zu = h + cond[p - 1, pl.ds(lo + r0, chunk)]
-        zd = h + cond[p + 1, pl.ds(lo + r0, chunk)]
-        cxl[p - 1, at] = xl
-        cxr[p - 1, at] = xr
-        cyu[p - 1, at] = yu
-        cyd[p - 1, at] = yd
-        cz[p - 1, at] = zu
-        cz[p, at] = zd
-        flat = (xl + xr) + (yu + yd)
-        for s in range(sections):
-            above, here, below = act[s]
-            diagonal = (LOSS_RATE * here + (1.0 - here)) + here * (flat + above * zu + below * zd)
-            inv = here / diagonal
-            g = inv * grad[s, p - 1, at]
-            inverse[s, p - 1, at] = inv
-            grad[s, p - 1, at] = g
-            first = g * (1.0 / CENTER)
-            update[s, p - 1, at] = first
-            field[1, s, p, pl.ds(lo + r0, chunk)] = first
+        hs = [cond[p, h, pl.ds(lo + r0, chunk)] for h in halves]
+        hl, hr = left(hs), right(hs)
+        for h in halves:
+            here_h = hs[h]
+            xl = here_h + hl[h]
+            xr = here_h + hr[h]
+            if h == 0:
+                xl = jnp.where(lane == 0, 0.0, xl)
+            if h == parts - 1:
+                xr = jnp.where(lane == lanes - 1, 0.0, xr)
+            yu = here_h + cond[p, h, pl.ds(lo + r0 - 1, chunk)]
+            yd = here_h + cond[p, h, pl.ds(lo + r0 + 1, chunk)]
+            if r0 == 0:
+                yu = yu * up_mask
+            if r0 == rows - chunk:
+                yd = yd * down_mask
+            zu = here_h + cond[p - 1, h, pl.ds(lo + r0, chunk)]
+            zd = here_h + cond[p + 1, h, pl.ds(lo + r0, chunk)]
+            cxl[p - 1, h, at] = xl
+            cxr[p - 1, h, at] = xr
+            cyu[p - 1, h, at] = yu
+            cyd[p - 1, h, at] = yd
+            cz[p - 1, h, at] = zu
+            cz[p, h, at] = zd
+            flat = (xl + xr) + (yu + yd)
+            for s in range(sections):
+                above, here, below = act[s]
+                diagonal = (LOSS_RATE * here + (1.0 - here)) + here * (
+                    flat + above * zu + below * zd
+                )
+                inv = here / diagonal
+                g = inv * grad[s, p - 1, h, at]
+                inverse[s, p - 1, h, at] = inv
+                grad[s, p - 1, h, at] = g
+                first = g * (1.0 / CENTER)
+                update[s, p - 1, h, at] = first
+                odd[s, p, h, pl.ds(lo + r0, chunk)] = first
 
     def start_edges(s, par):
         each(zsides, lambda side: vz_copy(side, s, par).start())
@@ -281,28 +304,33 @@
     def relax_plane(s, p, now, new, alpha, beta):
         for r0 in starts:
             at = pl.ds(r0, chunk)
-            v = field[now, s, p, pl.ds(lo + r0, chunk)]
-            total = cxl[p - 1, at] * left(v) + cxr[p - 1, at] * right(v)
-            total += cyu[p - 1, at] * field[now, s, p, pl.ds(lo + r0 - 1, chunk)]
-            total += cyd[p - 1, at] * field[now, s, p, pl.ds(lo + r0 + 1, chunk)]
-            total += cz[p - 1, at] * field[now, s, p - 1, pl.ds(lo + r0, chunk)]
-            total += cz[p, at] * field[now, s, p + 1, pl.ds(lo + r0, chunk)]
-            u = alpha * update[s, p - 1, at] + beta * (
-                (grad[s, p - 1, at] - v) + inverse[s, p - 1, at] * total
+            mid = pl.ds(lo + r0, chunk)
+            vs = [now[s, p, h, mid] for h in halves]
+            vl, vr = left(vs), right(vs)
+            for h in halves:
+                v = vs[h]
+                total = cxl[p - 1, h, at] * vl[h] + cxr[p - 1, h, at] * vr[h]
+                total += cyu[p - 1, h, at] * now[s, p, h, pl.ds(lo + r0 - 1, chunk)]
+                total += cyd[p - 1, h, at] * now[s, p, h, pl.ds(lo + r0 + 1, chunk)]
+                total += cz[p - 1, h, at] * now[s, p - 1, h, mid]
+                total += cz[p, h, at] * now[s, p + 1, h, mid]
+                u = alpha * update[s, p - 1, h, at] + beta * (
+                    (grad[s, p - 1, h, at] - v) + inverse[s, p - 1, h, at] * total
+                )
+                update[s, p - 1, h, at] = u
+                new[s, p, h, mid] = v + u
+
+    for n in range(2, SWEEPS + 1):
+        now, new = (n - 1) % 2, n % 2
+        for s in range(sections):
+            relax = functools.partial(
+                relax_plane, now=fields[now], new=fields[new], alpha=table[n - 2][0], beta=table[n - 2][1]
             )
-            update[s, p - 1, at] = u
-            field[new, s, p, pl.ds(lo + r0, chunk)] = v + u
-
-    def sweep(n, _):
-        now, new = lax.rem(n - 1, 2), lax.rem(n, 2)
-        alpha = pick(n - 2, [a for a, _ in table])
-        beta = pick(n - 2, [b for _, b in table])
-        for s in range(sections):
             each(zsides, lambda side: vz_copy(1 - side, s, now).wait_recv())
             each(ysides, lambda side: [vy_copy(1 - side, s, group, now).wait_recv() for group in (0, 1)])
 
             def edge(i, _):
-                relax_plane(s, 1 + i * (planes - 1), now, new, alpha, beta)
+                relax(s, 1 + i * (planes - 1))
                 return 0
 
             lax.fori_loop(0, 2, edge, 0)
@@ -311,7 +339,7 @@
                 each(ysides, lambda side: vy_copy(1 - side, s, 2, now).wait_recv())
 
                 def inner(p, _):
-                    relax_plane(s, p, now, new, alpha, beta)
+                    relax(s, p)
                     return 0
 
                 lax.fori_loop(2, planes, inner, 0)
@@ -319,13 +347,17 @@
                 each(ysides, lambda side: vy_copy(side, s, 2, now).wait_send())
             each(zsides, lambda side: vz_copy(side, s, now).wait_send())
             each(ysides, lambda side: [vy_copy(side, s, group, now).wait_send() for group in (0, 1)])
-        return 0
-
-    lax.fori_loop(2, SWEEPS + 1, sweep, 0)
 
     last = SWEEPS % 2
-    store = pltpu.make_async_copy(field.at[last, :, pl.ds(1, planes), body], adj_ref, store_sem)
-    store.start()
+    stores = [
+        pltpu.make_async_copy(
+            fields[last].at[:, pl.ds(1, planes), h, body],
+            adj_ref.at[:, :, :, pl.ds(h * lanes, lanes)], store_sem.at[h],
+        )
+        for h in halves
+    ]
+    for store in stores:
+        store.start()
 
     def ex_copy(k, p, slot):
         return remote(
@@ -335,40 +367,47 @@
 
     def energy_plane(p):
         for r0 in starts:
-            rest = jnp.zeros((chunk, cols), jnp.float32)
-            across = jnp.zeros((chunk, cols), jnp.float32)
+            rest = [0.0] * parts
+            across = [0.0] * parts
             for s in range(sections):
                 above, here, below = active[s][p - 1 : p + 2]
 
-                def both(plane, shift):
+                def both(plane, h, shift):
                     at = pl.ds(lo + r0 + shift, chunk)
-                    return field[last, s, plane, at], temp[s, plane, at]
-
-                v, t = both(p, 0)
-                across += here * ((v - left(v)) * (t - left(t)))
-                v2, t2 = both(p, -1)
-                term = (v - v2) * (t - t2)
-                if r0 == 0:
-                    term = term * up_mask
-                v2, t2 = both(p, 1)
-                more = (v - v2) * (t - t2)
-                if r0 == rows - chunk:
-                    more = more * down_mask
-                term += more
-                v2, t2 = both(p - 1, 0)
-                term += above * ((v - v2) * (t - t2))
-                v2, t2 = both(p + 1, 0)
-                term += below * ((v - v2) * (t - t2))
-                rest += here * term
-            across = jnp.where(lane == 0, 0.0, across)
-            total = 0.5 * (rest + (across + right(across)))
+                    return fields[last][s, plane, h, at], temp[s, plane, h, at]
+
+                pairs = [both(p, h, 0) for h in halves]
+                vl, tl = left([v for v, _ in pairs]), left([t for _, t in pairs])
+                for h in halves:
+                    v, t = pairs[h]
+                    across[h] += here * ((v - vl[h]) * (t - tl[h]))
+                    v2, t2 = both(p, h, -1)
+                    term = (v - v2) * (t - t2)
+                    if r0 == 0:
+                        term = term * up_mask
+                    v2, t2 = both(p, h, 1)
+                    more = (v - v2) * (t - t2)
+                    if r0 == rows - chunk:
+                        more = more * down_mask
+                    term += more
+                    v2, t2 = both(p - 1, h, 0)
+                    term += above * ((v - v2) * (t - t2))
+                    v2, t2 = both(p + 1, h, 0)
+                    term += below * ((v - v2) * (t - t2))
+                    rest[h] += here * term
+            across[0] = jnp.where(lane == 0, 0.0, across[0])
+            beyond = right(across)
+            beyond[-1] = jnp.where(lane == lanes - 1, 0.0, beyond[-1])
+            totals = [0.5 * (rest[h] + (across[h] + beyond[h])) for h in halves]
+            if width != lanes:
+                total = jnp.concatenate(totals, axis=-1)
+                totals = [total[:, k * width : (k + 1) * width] for k in range(nx)]
             for k in range(nx):
-                part_out[k, p - 1, pl.ds(r0, chunk)] = total[:, k * width : (k + 1) * width]
+                part_out[k, p - 1, pl.ds(r0, chunk)] = totals[k]
         for k in range(1, nx):
             ex_copy(k, p, (xpeer(k), me_x)).start()
 
     each(ysides, lambda side: ty_copy(1 - side).wait_recv())
-    load_t.wait()
     for s in range(sections):
         each(ysides, lambda side: [vy_copy(1 - side, s, g, last).wait_recv() for g in (0, 1)])
         if planes > 2:
@@ -405,7 +444,8 @@
         each(ysides, lambda side: [vy_copy(side, s, g, last).wait_send() for g in (0, 1)])
         if planes > 2:
             each(ysides, lambda side: vy_copy(side, s, 2, last).wait_send())
-    store.wait()
+    for store in stores:
+        store.wait()
 
 
 def solution(mesh):
@@ -417,8 +457,10 @@
         f32 = jnp.float32
         tall = rows + 2 * PAD
         dma = pltpu.SemaphoreType.DMA
-        inner = (planes, rows, cols)
-        anywhere = pl.BlockSpec(memory_space=pl.ANY)
+        lanes = 128 if cols % 128 == 0 else cols
+        split = cols // lanes
+        inner = (planes, split, rows, lanes)
+        anywhere = pl.BlockSpec(memory_space=pltpu.HBM)
         return pl.pallas_call(
             functools.partial(kernel, (nz, nx, ny, slice_to_deposit.shape[0])),
             out_shape=(
@@ -428,22 +470,23 @@
             in_specs=[anywhere] * 3 + [pl.BlockSpec(memory_space=pltpu.SMEM)] * 2,
             out_specs=(anywhere, pl.BlockSpec(memory_space=pltpu.VMEM)),
             scratch_shapes=[
-                pltpu.VMEM((2, sections, planes + 2, tall, cols), f32),
-                pltpu.VMEM((sections, planes + 2, tall, cols), f32),
+                pltpu.VMEM((sections, planes + 2, split, tall, lanes), f32),
+                pltpu.VMEM((sections, planes + 2, split, tall, lanes), f32),
+                pltpu.VMEM((sections, planes + 2, split, tall, lanes), f32),
                 pltpu.VMEM((sections,) + inner, f32),
                 pltpu.VMEM((sections,) + inner, f32),
                 pltpu.VMEM((sections,) + inner, f32),
-                pltpu.VMEM((planes + 2, tall, cols), f32),
+                pltpu.VMEM((planes + 2, split, tall, lanes), f32),
                 pltpu.VMEM((nx, planes + 2, tall, width), f32),
                 pltpu.VMEM(inner, f32),
                 pltpu.VMEM(inner, f32),
                 pltpu.VMEM(inner, f32),
                 pltpu.VMEM(inner, f32),
-                pltpu.VMEM((planes + 1, rows, cols), f32),
+                pltpu.VMEM((planes + 1, split, rows, lanes), f32),
                 pltpu.VMEM((nx, planes, rows, width), f32),
                 pltpu.VMEM((nx, planes, rows, width), f32),
-                dma((3,)),
-                dma(()),
+                dma((1 + 2 * split,)),
+                dma((split,)),
                 dma((nx,)), dma((nx,)),
                 dma((2, nx)), dma((2, nx)),
                 dma((2, nx)), dma((2, nx)),
@@ -454,7 +497,7 @@
                 dma((nx, planes)), dma((nx, planes)),
             ],
             compiler_params=pltpu.CompilerParams(
-                collective_id=0, has_side_effects=True, vmem_limit_bytes=40 * 1024 * 1024
+                collective_id=0, has_side_effects=True, vmem_limit_bytes=63 * 1024 * 1024
             ),
         )(material_share, stored_thermal_state, objective_slope, print_depths, slice_to_deposit)
 

time: 64.8 us -> 61.8 us (0.954)
  local copies, waits for them, and re-layouts: 6.38 us -> 3.02 us
    unnamed x12 -> x4, local copies, waits for them, and re-layouts: 6.38 us -> 3.02 us
where the time goes in v2:
time: 61.8 us; the launch traced here: 61.6 us
  Pallas kernels  57.9 us (94%)
  local copies, waits for them, and re-layouts  3.02 us (5%)
  between operations  0.65 us (1%)
    pallas_call x1, Pallas kernels, body(): pl.pallas_call(functools.partial(kernel, (nz, nx, ny, slice_to_deposit.sh...  57.9 us
    unnamed x4, local copies, waits for them, and re-layouts  3.02 us

profile of v2, /device:TPU:0, one launch (start us, length us, event | category | flops | bytes accessed | tf_op | source)
XLA Modules:
  0.0 61.6 jit_solution(8658091991274636406)
XLA Ops:
  0.6 57.9 %shard_map.68 = (f32[2,4,128,256]{3,2,1,0:T(8,128)}, f32[4,128,128]{2,1,0:T(8,128)}) custom-call(f32[4,128,128]{2,1,0:T(8,128)} %m_ref.1, f32[2,4,128,256]{3,2,1,0:T(8,128)} %t_ref.1, f32[2,4,128,256]{3,2,1,0:T(8,128)} %g_ref.1, s32[2]{0:T(128)} %depth_ref.1, s32[16]{0:T(128)} %layer_ref.1), custom_call_target="tpu_custom_call" | custom-call | tf_op jit(solution)/shard_map/pallas_call | solution.py:464
  58.6 0.0 copy-start
  58.6 2.3 %copy.9 = f32[2,4,128,256]{3,2,1,0:T(8,128)} copy(f32[2,4,128,256]{3,2,1,0:T(8,128)} %get-tuple-element.4) | data formatting | bytes 2097152
  60.9 0.0 copy-done
  60.9 0.7 %copy.10 = f32[4,128,128]{2,1,0:T(8,128)} copy(f32[4,128,128]{2,1,0:T(8,128)S(1)} %copy-done) | data formatting | bytes 524288
Async XLA Ops:
  58.6 2.3 %copy-start = (f32[4,128,128]{2,1,0:T(8,128)S(1)}, f32[4,128,128]{2,1,0:T(8,128)}, u32[]{:S(2)}) copy-start(f32[4,128,128]{2,1,0:T(8,128)} %get-tuple-element.5) | copy-start | bytes 786436

commit v3 on v2

--- a/solution.py
+++ b/solution.py
@@ -40,7 +40,7 @@
     mx_send, mx_recv, mz_send, mz_recv, my_send, my_recv,
     tz_send, tz_recv, ty_send, ty_recv,
     vz_send, vz_recv, vy_send, vy_recv,
-    ex_send, ex_recv,
+    ex_send, ex_recv, eq_send, eq_recv, vq_send, vq_recv,
 ):
     nz, nx, ny, total_planes = sizes
     sections, planes, rows, cols = t_ref.shape
@@ -161,6 +161,13 @@
         dst = fields[par].at[s, planes + 1 if side == 0 else 0, :, body]
         return remote(
             src, dst, vz_send.at[side, s, par], vz_recv.at[side, s, par], {"slab": zsides[side][2]}
+        )
+
+    def vq_copy(side, q):
+        here = fields[SWEEPS % 2].at[sections - 1, :, :, pl.ds(lo + starts[q], chunk)]
+        return remote(
+            here.at[1 if side == 0 else planes], here.at[planes + 1 if side == 0 else 0],
+            vq_send.at[side, q], vq_recv.at[side, q], {"slab": zsides[side][2]},
         )
 
     spans = [(1, 1), (planes, 1), (2, planes - 2)]
@@ -277,8 +284,14 @@
                 update[s, p - 1, h, at] = first
                 odd[s, p, h, pl.ds(lo + r0, chunk)] = first
 
-    def start_edges(s, par):
-        each(zsides, lambda side: vz_copy(side, s, par).start())
+    pieces = range(len(starts))
+
+    def start_edges(s, par, pieced=False):
+        if pieced:
+            for q in pieces:
+                each(zsides, lambda side: vq_copy(side, q).start())
+        else:
+            each(zsides, lambda side: vz_copy(side, s, par).start())
         each(ysides, lambda side: [vy_copy(side, s, group, par).start() for group in (0, 1)])
 
     def start_inner(s, par):
@@ -334,7 +347,7 @@
                 return 0
 
             lax.fori_loop(0, 2, edge, 0)
-            start_edges(s, new)
+            start_edges(s, new, n == SWEEPS and s == sections - 1)
             if planes > 2:
                 each(ysides, lambda side: vy_copy(1 - side, s, 2, now).wait_recv())
 
@@ -364,6 +377,33 @@
             part_out.at[slot[0], p - 1], part_in.at[slot[1], p - 1], ex_send.at[k, p - 1],
             ex_recv.at[slot[1], p - 1], {"section": xpeer(k)},
         )
+
+    def eq_copy(k, p, q, slot):
+        edge, at = 0 if p == 1 else 1, pl.ds(starts[q], chunk)
+        return remote(
+            part_out.at[slot[0], p - 1, at], part_in.at[slot[1], p - 1, at], eq_send.at[k, edge, q],
+            eq_recv.at[slot[1], edge, q], {"section": xpeer(k)},
+        )
+
+    def split_columns(totals):
+        if width == lanes:
+            return totals
+        total = jnp.concatenate(totals, axis=-1)
+        return [total[:, k * width : (k + 1) * width] for k in range(nx)]
+
+    def energy_outer(p, q, outer):
+        r0 = starts[q]
+        at = pl.ds(lo + r0, chunk)
+        totals = [0.0] * parts
+        for s in range(sections):
+            weight = 0.5 * active[s][p] * active[s][outer]
+            for h in halves:
+                dv = fields[last][s, p, h, at] - fields[last][s, outer, h, at]
+                totals[h] += weight * (dv * (temp[s, p, h, at] - temp[s, outer, h, at]))
+        for k, total in enumerate(split_columns(totals)):
+            part_out[k, p - 1, pl.ds(r0, chunk)] += total
+        for k in range(1, nx):
+            eq_copy(k, p, q, (xpeer(k), me_x)).start()
 
     def energy_plane(p):
         for r0 in starts:
@@ -390,21 +430,20 @@
                     if r0 == rows - chunk:
                         more = more * down_mask
                     term += more
-                    v2, t2 = both(p - 1, h, 0)
-                    term += above * ((v - v2) * (t - t2))
-                    v2, t2 = both(p + 1, h, 0)
-                    term += below * ((v - v2) * (t - t2))
+                    if p > 1:
+                        v2, t2 = both(p - 1, h, 0)
+                        term += above * ((v - v2) * (t - t2))
+                    if p < planes:
+                        v2, t2 = both(p + 1, h, 0)
+                        term += below * ((v - v2) * (t - t2))
                     rest[h] += here * term
             across[0] = jnp.where(lane == 0, 0.0, across[0])
             beyond = right(across)
             beyond[-1] = jnp.where(lane == lanes - 1, 0.0, beyond[-1])
             totals = [0.5 * (rest[h] + (across[h] + beyond[h])) for h in halves]
-            if width != lanes:
-                total = jnp.concatenate(totals, axis=-1)
-                totals = [total[:, k * width : (k + 1) * width] for k in range(nx)]
-            for k in range(nx):
-                part_out[k, p - 1, pl.ds(r0, chunk)] = totals[k]
-        for k in range(1, nx):
+            for k, total in enumerate(split_columns(totals)):
+                part_out[k, p - 1, pl.ds(r0, chunk)] = total
+        for k in range(1, nx if 1 < p < planes else 1):
             ex_copy(k, p, (xpeer(k), me_x)).start()
 
     each(ysides, lambda side: ty_copy(1 - side).wait_recv())
@@ -412,35 +451,54 @@
         each(ysides, lambda side: [vy_copy(1 - side, s, g, last).wait_recv() for g in (0, 1)])
         if planes > 2:
             each(ysides, lambda side: vy_copy(1 - side, s, 2, last).wait_recv())
+    for p in list(range(2, planes)) + [1, planes]:
+        energy_plane(p)
+
+    def finish(p, r0, number):
+        at = pl.ds(r0, number)
+        total = part_out[me_x, p - 1, at]
+        for k in range(1, nx):
+            total += part_in[xpeer(k), p - 1, at]
+        m = share[me_x, p, pl.ds(lo + r0, number)]
+        sens_ref[p - 1, at] = (-(1.0 - FLOOR_COND) * SIMP_POWER) * (m * m) * total
+
     for p in range(2, planes):
-        energy_plane(p)
-    each(zsides, lambda side: tz_copy(1 - side).wait_recv())
-    for s in range(sections):
-        each(zsides, lambda side: vz_copy(1 - side, s, last).wait_recv())
-    energy_plane(1)
-    energy_plane(planes)
-
-    for p in list(range(2, planes)) + [1, planes]:
         for k in range(1, nx):
             ex_copy(k, p, (xpeer(k), xpeer(k))).wait_recv()
         for r0 in starts:
-            at = pl.ds(r0, chunk)
-            total = part_out[me_x, p - 1, at]
+            finish(p, r0, chunk)
+
+    each(zsides, lambda side: tz_copy(1 - side).wait_recv())
+    for s in range(sections - 1):
+        each(zsides, lambda side: vz_copy(1 - side, s, last).wait_recv())
+    for q in pieces:
+        each(zsides, lambda side: vq_copy(1 - side, q).wait_recv())
+        energy_outer(1, q, 0)
+        energy_outer(planes, q, planes + 1)
+
+    for q in pieces:
+        for p in (1, planes):
             for k in range(1, nx):
-                total += part_in[xpeer(k), p - 1, at]
-            m = share[me_x, p, pl.ds(lo + r0, chunk)]
-            sens_ref[p - 1, at] = (-(1.0 - FLOOR_COND) * SIMP_POWER) * (m * m) * total
+                eq_copy(k, p, q, (xpeer(k), xpeer(k))).wait_recv()
+            finish(p, starts[q], chunk)
 
     for k in range(1, nx):
         mx_copy(k, me_x).wait_send()
-        for p in range(1, planes + 1):
+        for p in range(2, planes):
             ex_copy(k, p, (xpeer(k), me_x)).wait_send()
+        for q in pieces:
+            for p in (1, planes):
+                eq_copy(k, p, q, (xpeer(k), me_x)).wait_send()
     each(ysides, lambda side: [my_copy(side, k, me_x).wait_send() for k in range(nx)])
     each(zsides, lambda side: [mz_copy(side, k, me_x).wait_send() for k in range(nx)])
     each(ysides, lambda side: ty_copy(side).wait_send())
     each(zsides, lambda side: tz_copy(side).wait_send())
     for s in range(sections):
-        each(zsides, lambda side: vz_copy(side, s, last).wait_send())
+        if s < sections - 1:
+            each(zsides, lambda side: vz_copy(side, s, last).wait_send())
+        else:
+            for q in pieces:
+                each(zsides, lambda side: vq_copy(side, q).wait_send())
         each(ysides, lambda side: [vy_copy(side, s, g, last).wait_send() for g in (0, 1)])
         if planes > 2:
             each(ysides, lambda side: vy_copy(side, s, 2, last).wait_send())
@@ -459,6 +517,7 @@
         dma = pltpu.SemaphoreType.DMA
         lanes = 128 if cols % 128 == 0 else cols
         split = cols // lanes
+        steps = rows // min(32, rows)
         inner = (planes, split, rows, lanes)
         anywhere = pl.BlockSpec(memory_space=pltpu.HBM)
         return pl.pallas_call(
@@ -495,6 +554,8 @@
                 dma((2, sections, 2)), dma((2, sections, 2)),
                 dma((2, sections, 3, 2)), dma((2, sections, 3, 2)),
                 dma((nx, planes)), dma((nx, planes)),
+                dma((nx, 2, steps)), dma((nx, 2, steps)),
+                dma((2, steps)), dma((2, steps)),
             ],
             compiler_params=pltpu.CompilerParams(
                 collective_id=0, has_side_effects=True, vmem_limit_bytes=63 * 1024 * 1024

time: 61.8 us -> 63.2 us (1.023)
  Pallas kernels: 57.9 us -> 59.4 us
    pallas_call x1, Pallas kernels: 57.9 us -> 59.4 us  [body(): pl.pallas_call(functools.partial(kernel, (nz, nx, ny, slice_to_deposit.sh...]
where the time goes in v3:
time: 63.2 us; the launch traced here: 63.1 us
  Pallas kernels  59.4 us (94%)
  local copies, waits for them, and re-layouts  3.02 us (5%)
  between operations  0.65 us (1%)
    pallas_call x1, Pallas kernels, body(): pl.pallas_call(functools.partial(kernel, (nz, nx, ny, slice_to_deposit.sh...  59.4 us
    unnamed x4, local copies, waits for them, and re-layouts  3.02 us

profile of v3, /device:TPU:0, one launch (start us, length us, event | category | flops | bytes accessed | tf_op | source)
XLA Modules:
  0.0 63.1 jit_solution(15792547725396727951)
XLA Ops:
  0.6 59.4 %shard_map.68 = (f32[2,4,128,256]{3,2,1,0:T(8,128)}, f32[4,128,128]{2,1,0:T(8,128)}) custom-call(f32[4,128,128]{2,1,0:T(8,128)} %m_ref.1, f32[2,4,128,256]{3,2,1,0:T(8,128)} %t_ref.1, f32[2,4,128,256]{3,2,1,0:T(8,128)} %g_ref.1, s32[2]{0:T(128)} %depth_ref.1, s32[16]{0:T(128)} %layer_ref.1), custom_call_target="tpu_custom_call" | custom-call | tf_op jit(solution)/shard_map/pallas_call | solution.py:523
  60.1 0.0 copy-start
  60.1 2.3 %copy.9 = f32[2,4,128,256]{3,2,1,0:T(8,128)} copy(f32[2,4,128,256]{3,2,1,0:T(8,128)} %get-tuple-element.4) | data formatting | bytes 2097152
  62.4 0.0 copy-done
  62.4 0.7 %copy.10 = f32[4,128,128]{2,1,0:T(8,128)} copy(f32[4,128,128]{2,1,0:T(8,128)S(1)} %copy-done) | data formatting | bytes 524288
Async XLA Ops:
  60.1 2.3 %copy-start = (f32[4,128,128]{2,1,0:T(8,128)S(1)}, f32[4,128,128]{2,1,0:T(8,128)}, u32[]{:S(2)}) copy-start(f32[4,128,128]{2,1,0:T(8,128)} %get-tuple-element.5) | copy-start | bytes 786436
